TPU v7x, 32 devices: a whole 2x2x4 slice. The times are simulated.
32 devices in a mesh: groups: 2 (over y), tile: 4 (over z), pair: 2 (over x), sub: 2 (over core).
Axes of the slice: x: 2, y: 2, z: 4, core: 2. Of those that a mesh axis runs over, the one named last changes fastest.
Arguments:
- ref_chips: bfloat16 [4, 256, 4096], P(('groups', 'pair'), ('tile', 'sub')), parts along dimension 0, may hold values from -300 to 700
- search_windows: bfloat16 [4, 512, 16384], P(('groups', 'pair'), ('tile', 'sub')), parts along dimension 0, may hold values from -300 to 700
- dest_block: int32 [4, 512, 1], P(('groups', 'pair'), ('tile', 'sub')), parts along dimension 0, may hold values from 0 to 7; in each aligned block of 64 rows (0 to 63, 64 to 127, ..., all dimensions but the last counted through in order) at most 16 rows name the same one
- dest_slot: int32 [4, 512], P(('groups', 'pair'), ('tile', 'sub')), parts along dimension 0, may hold values from 0 to 31
Outputs:
- smoothed_scores: float32 [4, 256, 4096], P(('groups', 'pair'), ('tile', 'sub')), parts along dimension 0
There are 2 independent parts, one for each index of `groups`. A program takes and returns all parts, laid end to end along the dimension named above; each array names one. Nothing has to cross between parts.
Inputs may be any that keep to these rules, and one draw needn't show every extreme that they name: `dest_block`: in the rows of one device (aligned blocks of 64 windows), no block index is named by more than 16 windows.
All inputs are finite; a program needn't handle non-finite values.
Results may differ from a plain program's by a relative error of at most 0.0003.
Values may be sent and summed in bfloat16 or wider, within the bound.
A program may use at most 64 MiB of HBM per device.

v0:
```python
import math

import jax
import jax.numpy as jnp
from jax import lax
from jax.sharding import PartitionSpec as P

CHIP = 64
WIN = 128
GC = 8


precise = lax.Precision.HIGHEST
epsilon = 1e-06


def padded(block, sides, width):
    for axis, dim in sides:
        count = lax.axis_size(axis)
        forward = [(i, i + 1) for i in range(count - 1)]
        backward = [(target, source) for source, target in forward]
        low = lax.ppermute(
            lax.slice_in_dim(block, block.shape[dim] - width, None, axis=dim), axis, forward
        )
        high = lax.ppermute(lax.slice_in_dim(block, 0, width, axis=dim), axis, backward)
        block = jnp.concatenate([low, block, high], axis=dim)
    return block


def tables(length, width):
    freqs = jnp.arange(length, dtype=jnp.int32)[:, None]
    places = jnp.arange(width, dtype=jnp.int32)[None, :]
    phase = freqs * places % length
    angle = phase.astype(jnp.float32) * (2.0 * math.pi / length)
    return (jnp.cos(angle), jnp.sin(angle))


def spectrum(image, cosine, sine_table):
    first_real = jnp.einsum("kn,bnm->bkm", cosine, image, precision=precise)
    first_imag = -jnp.einsum("kn,bnm->bkm", sine_table, image, precision=precise)
    spec_real = jnp.einsum("bkm,lm->bkl", first_real, cosine, precision=precise) + jnp.einsum(
        "bkm,lm->bkl", first_imag, sine_table, precision=precise
    )
    spec_imag = jnp.einsum("bkm,lm->bkl", first_imag, cosine, precision=precise) - jnp.einsum(
        "bkm,lm->bkl", first_real, sine_table, precision=precise
    )
    return (spec_real, spec_imag)


def centre(chips_raw, chip_side):
    chip_float = chips_raw.astype(jnp.float32).reshape(-1, chip_side, chip_side)
    centred = chip_float - jnp.mean(chip_float, axis=(1, 2), keepdims=True)
    chip_std = jnp.sqrt(jnp.mean(centred * centred, axis=(1, 2)) + epsilon)
    return (centred, chip_std)


def match(chip_real, chip_imag, chip_std, windows_raw, chip_side, window_side):
    offsets = window_side - chip_side
    cos_full, sin_full = tables(window_side, window_side)
    cos_part = cos_full[:offsets]
    sin_part = sin_full[:offsets]
    window_float = windows_raw.astype(jnp.float32).reshape(-1, window_side, window_side)
    win_real, win_imag = spectrum(window_float, cos_full, sin_full)
    product_real = chip_real * win_real + chip_imag * win_imag
    product_imag = chip_real * win_imag - chip_imag * win_real
    half_real = jnp.einsum("ak,bkl->bal", cos_part, product_real, precision=precise) - jnp.einsum(
        "ak,bkl->bal", sin_part, product_imag, precision=precise
    )
    half_imag = jnp.einsum("ak,bkl->bal", cos_part, product_imag, precision=precise) + jnp.einsum(
        "ak,bkl->bal", sin_part, product_real, precision=precise
    )
    numerator = (
        jnp.einsum("bal,el->bae", half_real, cos_part, precision=precise)
        - jnp.einsum("bal,el->bae", half_imag, sin_part, precision=precise)
    ) / (window_side * window_side)
    starts = jnp.arange(offsets, dtype=jnp.int32)[:, None]
    pixels = jnp.arange(window_side, dtype=jnp.int32)[None, :]
    window_band = ((pixels >= starts) & (pixels < starts + chip_side)).astype(jnp.float32)
    first_rows = jnp.einsum("ax,bxy->bay", window_band, window_float, precision=precise)
    first_sum = jnp.einsum("bay,ey->bae", first_rows, window_band, precision=precise)
    second_rows = jnp.einsum(
        "ax,bxy->bay", window_band, window_float * window_float, precision=precise
    )
    second_sum = jnp.einsum("bay,ey->bae", second_rows, window_band, precision=precise)
    patch_mean = first_sum / (chip_side * chip_side)
    patch_var = second_sum / (chip_side * chip_side) - patch_mean * patch_mean
    score = numerator / (chip_side * chip_std[:, None, None] * jnp.sqrt(patch_var + epsilon))
    return score.reshape(-1, offsets * offsets)


def in_blocks(function, operands):
    amount = operands[0].shape[0]
    block_rows = 16
    shaped = tuple(
        (item.reshape((amount // block_rows, block_rows) + item.shape[1:]) for item in operands)
    )
    result = lax.map(lambda grouped: function(*grouped), shaped)
    return result.reshape(amount, -1)


def on_device(ref_chips, search_windows, dest_block, dest_slot):
    chips = ref_chips[0]
    windows = search_windows[0]
    targets = dest_block[0, :, 0]
    target_slot = dest_slot[0]
    chip_side = CHIP
    window_side = WIN
    offsets = window_side - chip_side
    window_amount = windows.shape[0]
    chip_amount = chips.shape[0]
    devices = lax.axis_size(("tile", "sub"))
    capacity = max(2, 2 * window_amount // devices)
    slot_amount = devices * capacity
    order = jnp.arange(window_amount, dtype=jnp.int32)
    matches = targets[:, None] == targets[None, :]
    earlier = order[:, None] > order[None, :]
    ranking = jnp.sum((matches & earlier).astype(jnp.int32), axis=1)
    positions = targets * capacity + ranking
    slot_buffer = jnp.full((slot_amount,), -1, jnp.int32).at[positions].set(target_slot)
    cos_chip, sin_chip = tables(window_side, chip_side)
    requests = slot_buffer.reshape(devices, capacity)
    found = jnp.take(
        chips,
        jnp.maximum(
            lax.all_to_all(requests, ("tile", "sub"), split_axis=0, concat_axis=0, tiled=True), 0
        ),
        axis=0,
    )
    fetched = lax.all_to_all(found, ("tile", "sub"), split_axis=0, concat_axis=0, tiled=True)
    own_chips = jnp.take(fetched.reshape(slot_amount, chip_side * chip_side), positions, axis=0)

    def match_own(chip_part, window_part):
        centred_part, std_part = centre(chip_part, chip_side)
        real_part, imag_part = spectrum(centred_part, cos_chip, sin_chip)
        return match(real_part, imag_part, std_part, window_part, chip_side, window_side)

    own_scores = in_blocks(match_own, (own_chips, windows))
    score_buffer = (
        jnp.zeros((slot_amount, offsets * offsets), jnp.float32).at[positions].set(own_scores)
    )
    scores, slots_here = (
        lax.all_to_all(score_buffer, ("tile", "sub"), split_axis=0, concat_axis=0, tiled=True),
        lax.all_to_all(slot_buffer, ("tile", "sub"), split_axis=0, concat_axis=0, tiled=True),
    )
    hits_table = (slots_here[None, :] == jnp.arange(chip_amount, dtype=jnp.int32)[:, None]).astype(
        jnp.float32
    )
    total = jnp.dot(hits_table, scores, precision=precise)
    looks = jnp.sum(hits_table, axis=1)
    average = total / jnp.maximum(looks, 1.0)[:, None]
    grid = average.reshape(-1, GC, offsets * offsets)
    extended = padded(grid, ((("tile", "sub"), 0),), 1)
    vertical = extended[:-2] + extended[2:]
    sideways = jnp.pad(grid, ((0, 0), (1, 1), (0, 0)))
    horizontal = sideways[:, :-2] + sideways[:, 2:]
    smoothed = (4.0 * grid + vertical + horizontal) / 8.0
    return smoothed.reshape(1, chip_amount, offsets * offsets)


def solution(mesh):
    return jax.shard_map(
        on_device,
        mesh=mesh,
        in_specs=(
            P(("groups", "pair"), ("tile", "sub"), None),
            P(("groups", "pair"), ("tile", "sub"), None),
            P(("groups", "pair"), ("tile", "sub"), None),
            P(("groups", "pair"), ("tile", "sub")),
        ),
        out_specs=P(("groups", "pair"), ("tile", "sub"), None),
        check_vma=False,
    )
```

profile of v0, /device:TPU:1, one launch (start us, length us, event | category | flops | bytes accessed | tf_op | source)
XLA Modules:
  0.0 226.3 jit_solution(14719844709658617581)
XLA Ops:
  2.6 11.0 %all_to_all.35 = s32[8,1,16]{2,1,0:T(1,128)S(1)} all-to-all(s32[8,1,16]{2,1,0:T(1,128)S(1)} %bitcast.236), channel_id=1, replica_groups=mesh['groups'=2,'tile'=4,'pair'=2,'sub'=2] {'tile','sub'}, dimensions={0} | all-to-all | bytes 1024 | tf_op jit(solution)/shard_map/all_to_all | solution.py:125
  16.1 4.2 %all-to-all-start.2 = ((bf16[8,16,4096]{2,1,0:T(8,128)(2,1)}), bf16[8,16,4096]{2,1,0:T(8,128)(2,1)S(1)}, u32[]{:S(2)}, u32[]{:S(2)}) async-start(bf16[8,16,4096]{2,1,0:T(8,128)(2,1)} %broadcast_select_fusion), calls=%async_computation.2 | async-start | bytes 2097152 | tf_op jit(solution)/shard_map/all_to_all | solution.py:129
  21.1 24.9 %all-to-all-done.2 = bf16[8,16,4096]{2,1,0:T(8,128)(2,1)S(1)} async-done(((bf16[8,16,4096]{2,1,0:T(8,128)(2,1)}), bf16[8,16,4096]{2,1,0:T(8,128)(2,1)S(1)}, u32[]{:S(2)}, u32[]{:S(2)}) %all-to-all-start.2) | async-done | bytes 1048608 | tf_op jit(solution)/shard_map/all_to_all | solution.py:129
  46.0 4.1 %all-to-all-start = ((s32[8,16,1]{1,2,0:T(1,128)}), s32[8,16,1]{1,2,0:T(1,128)S(1)}, u32[]{:S(2)}, u32[]{:S(2)}) async-start(s32[8,16,1]{1,2,0:T(1,128)} %bitcast.5), calls=%async_computation | async-start | bytes 8192 | tf_op jit(solution)/shard_map/all_to_all | solution.py:143
  51.1 109.2 %while.14 = (s32[]{:T(128)}, f32[4,16,4096]{2,1,0:T(8,128)S(1)}, bf16[4,16,4096]{2,1,0:T(8,128)(2,1)S(1)}, bf16[4,16,16384]{2,1,0:T(8,128)(2,1)}, s32[]{:T(128)}) while((s32[]{:T(128)}, f32[4,16,4096]{2,1,0:T(8,128)S(1)}, bf16[4,16,4096]{2,1,0:T(8,128)(2,1)S(1)}, bf16[4,16,16384]{2,1,0:T(8,128)(2,1)}, s32[]{:T(128)}) %tuple.39), condition=%wide.region_5.6_spmd.clone.clone, body=%wide.region_2.5_spmd.clone.clone.sunk | while | flops 4872994816 | bytes 46598104 | solution.py:97
  58.2 2.0 fusion.248
  60.1 1.9 convolution_add_fusion.5
  62.1 1.9 fusion.252
  64.0 1.9 convolution_subtract_fusion.5
  71.5 1.9 multiply_subtract_fusion.2
  85.4 2.0 fusion.248
  87.4 1.9 convolution_add_fusion.5
  89.3 1.9 fusion.252
  91.3 1.9 convolution_subtract_fusion.5
  98.7 1.9 multiply_subtract_fusion.2
  112.7 2.0 fusion.248
  114.6 1.9 convolution_add_fusion.5
  116.6 1.9 fusion.252
  118.5 1.9 convolution_subtract_fusion.5
  122.3 1.8 convolution_add_fusion.6
  126.0 1.9 multiply_subtract_fusion.2
  139.9 2.0 fusion.248
  141.9 1.9 convolution_add_fusion.5
  143.8 1.9 fusion.252
  145.8 1.9 convolution_subtract_fusion.5
  153.2 1.9 multiply_subtract_fusion.2
  160.3 2.6 %scatter_custom_fusion.1 = f32[128,4096]{1,0:T(8,128)} fusion(s32[64]{0:T(128)S(1)} %fusion.136, f32[64,4096]{1,0:T(8,128)S(1)} %bitcast.237, f32[]{:T(128)} %constant.141.clone.1), kind=kCustom, calls=%fused_computation.150 | custom fusion | bytes 2097156 | tf_op jit(solution)/shard_map/scatter | solution.py:139
  162.9 5.1 %all-to-all-start.3 = ((f32[8,16,4096]{2,1,0:T(8,128)}), f32[8,16,4096]{2,1,0:T(8,128)S(1)}, u32[]{:S(2)}, u32[]{:S(2)}) async-start(f32[8,16,4096]{2,1,0:T(8,128)} %bitcast.15), calls=%async_computation.3 | async-start | bytes 4194304 | tf_op jit(solution)/shard_map/all_to_all | solution.py:142
  169.4 46.8 %all-to-all-done.3 = f32[8,16,4096]{2,1,0:T(8,128)S(1)} async-done(((f32[8,16,4096]{2,1,0:T(8,128)}), f32[8,16,4096]{2,1,0:T(8,128)S(1)}, u32[]{:S(2)}, u32[]{:S(2)}) %all-to-all-start.3) | async-done | bytes 2097184 | tf_op jit(solution)/shard_map/all_to_all | solution.py:142
  217.1 1.9 collective-permute-start
  219.0 2.4 %collective-permute-start.1 = (f32[1,8,4096]{2,1,0:T(8,128)S(1)}, f32[1,8,4096]{2,1,0:T(8,128)S(1)}, u32[]{:S(2)}, u32[]{:S(2)}) collective-permute-start(f32[1,8,4096]{2,1,0:T(8,128)S(1)} %get-tuple-element.139), channel_id=1, source_target_pairs={{1,0},{4,1},{5,4},{8,5},{9,8},{12,9},{13,12},{3,2},{6,3},{7,6},{10... | collective-permute-start | bytes 393224 | tf_op jit(solution)/shard_map/ppermute | solution.py:25
  221.5 3.9 %collective-permute-done.1 = f32[1,8,4096]{2,1,0:T(8,128)S(1)} collective-permute-done((f32[1,8,4096]{2,1,0:T(8,128)S(1)}, f32[1,8,4096]{2,1,0:T(8,128)S(1)}, u32[]{:S(2)}, u32[]{:S(2)}) %collective-permute-start.1) | collective-permute-done | bytes 131104 | tf_op jit(solution)/shard_map/ppermute | solution.py:25
  (156 shorter events, 77.5 us)
Async XLA Ops:
  0.0 13.7 %copy-start = (bf16[1,32,4096]{2,1,0:T(8,128)(2,1)S(1)}, bf16[1,32,4096]{2,1,0:T(8,128)(2,1)}, u32[]{:S(2)}) copy-start(bf16[1,32,4096]{2,1,0:T(8,128)(2,1)} %param.6) | copy-start | bytes 786436
  14.9 6.1 %copy-start.1 = (s32[1,64,1]{1,2,0:T(1,128)S(1)}, s32[1,64,1]{1,2,0:T(1,128)}, u32[]{:S(2)}) copy-start(s32[1,64,1]{1,2,0:T(1,128)} %param.8) | copy-start | bytes 772
  16.1 29.9 %all-to-all-start.2 = ((bf16[8,16,4096]{2,1,0:T(8,128)(2,1)}), bf16[8,16,4096]{2,1,0:T(8,128)(2,1)S(1)}, u32[]{:S(2)}, u32[]{:S(2)}) async-start(bf16[8,16,4096]{2,1,0:T(8,128)(2,1)} %broadcast_select_fusion), calls=%async_computation.2 | async-start | bytes 2097152 | tf_op jit(solution)/shard_map/all_to_all | solution.py:129
  46.0 116.9 %all-to-all-start = ((s32[8,16,1]{1,2,0:T(1,128)}), s32[8,16,1]{1,2,0:T(1,128)S(1)}, u32[]{:S(2)}, u32[]{:S(2)}) async-start(s32[8,16,1]{1,2,0:T(1,128)} %bitcast.5), calls=%async_computation | async-start | bytes 8192 | tf_op jit(solution)/shard_map/all_to_all | solution.py:143
  162.9 53.3 %all-to-all-start.3 = ((f32[8,16,4096]{2,1,0:T(8,128)}), f32[8,16,4096]{2,1,0:T(8,128)S(1)}, u32[]{:S(2)}, u32[]{:S(2)}) async-start(f32[8,16,4096]{2,1,0:T(8,128)} %bitcast.15), calls=%async_computation.3 | async-start | bytes 4194304 | tf_op jit(solution)/shard_map/all_to_all | solution.py:142
  217.1 4.3 %collective-permute-start = (f32[1,8,4096]{2,1,0:T(8,128)S(1)}, f32[1,8,4096]{2,1,0:T(8,128)S(1)}, u32[]{:S(2)}, u32[]{:S(2)}) collective-permute-start(f32[1,8,4096]{2,1,0:T(8,128)S(1)} %get-tuple-element.138), channel_id=1, source_target_pairs={{0,1},{1,4},{4,5},{5,8},{8,9},{9,12},{12,13},{2,3},{3,6},{6,7},{7,... | collective-permute-start | bytes 393224 | tf_op jit(solution)/shard_map/ppermute | solution.py:22
  219.0 6.3 %collective-permute-start.1 = (f32[1,8,4096]{2,1,0:T(8,128)S(1)}, f32[1,8,4096]{2,1,0:T(8,128)S(1)}, u32[]{:S(2)}, u32[]{:S(2)}) collective-permute-start(f32[1,8,4096]{2,1,0:T(8,128)S(1)} %get-tuple-element.139), channel_id=1, source_target_pairs={{1,0},{4,1},{5,4},{8,5},{9,8},{12,9},{13,12},{3,2},{6,3},{7,6},{10... | collective-permute-start | bytes 393224 | tf_op jit(solution)/shard_map/ppermute | solution.py:25
where the time goes:
time: 227 us; the launch traced here: 226 us
  matrix products  98 us (43%)
  waiting for transfers between devices  75.5 us (33%)
  starting transfers between devices  17.7 us (8%)
  local copies, waits for them, and re-layouts  14.4 us (6%)
  blocking collectives  11 us (5%)
  other arithmetic  8.43 us (4%)
    all_to_all x1, waiting for transfers between devices, on_device(): lax.all_to_all(score_buffer, ('tile', 'sub'), split_axis=0, concat_axis=0...  46.8 us
    all_to_all x1, waiting for transfers between devices, on_device(): lax.all_to_all(found, ('tile', 'sub'), split_axis=0, concat_axis=0, tiled...  24.9 us
    dot_general x8, matrix products, spectrum(): jnp.einsum('bkm,lm->bkl', first_real, sine_table, precision=precise)  15.5 us
    dot_general x8, matrix products, spectrum(): jnp.einsum('bkm,lm->bkl', first_real, cosine, precision=precise)  15.1 us
    dot_general x8, matrix products, spectrum(): jnp.einsum('bkm,lm->bkl', first_imag, sine_table, precision=precise)  15.1 us
    dot_general x8, matrix products, spectrum(): jnp.einsum('bkm,lm->bkl', first_imag, cosine, precision=precise)  15 us
    all_to_all x1, blocking collectives, on_device(): lax.all_to_all(requests, ('tile', 'sub'), split_axis=0, concat_axis=0, ti...  11 us
    dot_general x8, matrix products, spectrum(): first_real = jnp.einsum('kn,bnm->bkm', cosine, image, precision=precise)  6.31 us
  transfers between devices with their start and end apart: 5, of which 3 were waited for; matrix products, arithmetic and copies ran while one was open for 50% of the time, Pallas kernels for 0%

commit v1 on v0

v1 whole, which is shorter than its diff:
```python
import functools

import jax
import jax.numpy as jnp
from jax import lax
from jax.experimental import pallas as pl
from jax.experimental.pallas import tpu as pltpu
from jax.sharding import PartitionSpec as P

CHIP = 64
WIN = 128
GC = 8
LANES = 128
SUBLANES = 8
PHASES = 4
DEPTH = 80
EACH = 2

epsilon = 1e-06


def padded(block, sides, width):
    for axis, dim in sides:
        count = lax.axis_size(axis)
        forward = [(i, i + 1) for i in range(count - 1)]
        backward = [(target, source) for source, target in forward]
        low = lax.ppermute(
            lax.slice_in_dim(block, block.shape[dim] - width, None, axis=dim), axis, forward
        )
        high = lax.ppermute(lax.slice_in_dim(block, 0, width, axis=dim), axis, backward)
        block = jnp.concatenate([low, block, high], axis=dim)
    return block


def box_sums(image):
    step = 1
    while step < CHIP:
        image = image + pltpu.roll(image, WIN - step, 0)
        step *= 2
    image = image[:CHIP]
    step = 1
    while step < CHIP:
        image = image + pltpu.roll(image, WIN - step, 1)
        step *= 2
    return image


def correlate(chip_ref, window_ref, even_ref, odd_ref):
    chip = chip_ref.astype(jnp.float32)
    total = jnp.sum(jnp.sum(chip, axis=0, keepdims=True), axis=1, keepdims=True)
    mean = total / (CHIP * CHIP)
    centred = chip - mean
    square = jnp.sum(jnp.sum(centred * centred, axis=0, keepdims=True), axis=1, keepdims=True)
    chip_std = jnp.sqrt(square / (CHIP * CHIP) + epsilon)

    wide = jnp.concatenate([chip, jnp.zeros((CHIP, LANES - CHIP), jnp.float32)], axis=1)
    left = []
    for phase in range(PHASES):
        rows = []
        for v in range(phase, CHIP, PHASES):
            row = jnp.broadcast_to(wide[v : v + 1], (SUBLANES, LANES))
            rows.append(pltpu.roll(row, 0, 1, stride=1, stride_axis=0))
        left.append(jnp.concatenate(rows, axis=0).astype(jnp.bfloat16)[:, :DEPTH])
    left = jnp.concatenate(left, axis=1)

    window = window_ref.astype(jnp.float32)
    for phase in range(PHASES):
        moved = window if phase == 0 else pltpu.roll(window, WIN - phase, 1)
        even_ref[phase] = moved.astype(jnp.bfloat16)
        odd_ref[phase] = pltpu.roll(moved, WIN - SUBLANES, 0).astype(jnp.bfloat16)

    groups = CHIP // SUBLANES
    surfaces = []
    for pair in range(groups // 2):
        start = 2 * SUBLANES * pair
        right = jnp.concatenate(
            [
                jnp.concatenate([ref[phase, start : start + DEPTH] for phase in range(PHASES)], axis=0)
                for ref in (even_ref, odd_ref)
            ],
            axis=1,
        )
        partial = jnp.dot(left, right, preferred_element_type=jnp.float32)
        for half in range(2):
            part = partial[:, half * LANES : (half + 1) * LANES]
            value = part[:SUBLANES]
            for far in range(1, CHIP // PHASES):
                rows = part[far * SUBLANES : (far + 1) * SUBLANES]
                value = value + pltpu.roll(rows, LANES - PHASES * far, 1)
            surfaces.append(value)
    raw = jnp.concatenate(surfaces, axis=0)

    first = box_sums(window)
    second = box_sums(window * window)
    patch_mean = first / (CHIP * CHIP)
    patch_var = second / (CHIP * CHIP) - patch_mean * patch_mean
    numerator = raw - mean * first
    return numerator / (CHIP * chip_std * jnp.sqrt(patch_var + epsilon))


def match_kernel(places_ref, chips_ref, windows_ref, out_ref, even_ref, odd_ref):
    step = pl.program_id(0)

    @pl.when(step == 0)
    def _():
        out_ref[...] = jnp.zeros_like(out_ref)

    for item in range(EACH):
        score = correlate(chips_ref[item], windows_ref[item], even_ref.at[item], odd_ref.at[item])
        half = CHIP // 2
        low, high = score[:half], pltpu.roll(score[half:], CHIP, 1)
        lane = lax.broadcasted_iota(jnp.int32, (half, LANES), 1)
        out_ref[places_ref[step * EACH + item]] = jnp.where(lane < CHIP, low, high)


def match(positions, chips, windows, slot_amount):
    amount = windows.shape[0]
    half = CHIP // 2
    return pl.pallas_call(
        match_kernel,
        out_shape=jax.ShapeDtypeStruct((slot_amount, half, LANES), jnp.float32),
        grid_spec=pltpu.PrefetchScalarGridSpec(
            num_scalar_prefetch=1,
            grid=(amount // EACH,),
            in_specs=[
                pl.BlockSpec((EACH, CHIP, CHIP), lambda i, p: (i, 0, 0)),
                pl.BlockSpec((EACH, WIN, WIN), lambda i, p: (i, 0, 0)),
            ],
            out_specs=pl.BlockSpec((slot_amount, half, LANES), lambda i, p: (0, 0, 0)),
            scratch_shapes=[
                pltpu.VMEM((EACH, PHASES, WIN, LANES), jnp.bfloat16),
                pltpu.VMEM((EACH, PHASES, WIN, LANES), jnp.bfloat16),
            ],
        ),
        compiler_params=pltpu.CompilerParams(vmem_limit_bytes=40 * 1024 * 1024),
        cost_estimate=pl.CostEstimate(
            flops=amount * 2 * 128 * 512 * 1024, bytes_accessed=8 * 1024 * 1024, transcendentals=0
        ),
    )(positions, chips, windows)


def on_device(ref_chips, search_windows, dest_block, dest_slot):
    axes = ("tile", "sub")
    chips = ref_chips[0]
    windows = search_windows[0]
    targets = dest_block[0, :, 0]
    target_slot = dest_slot[0]
    window_amount = windows.shape[0]
    chip_amount = chips.shape[0]
    devices = lax.axis_size(axes)
    capacity = max(2, 2 * window_amount // devices)
    slot_amount = devices * capacity
    order = jnp.arange(window_amount, dtype=jnp.int32)
    matches = targets[:, None] == targets[None, :]
    earlier = order[:, None] > order[None, :]
    ranking = jnp.sum((matches & earlier).astype(jnp.int32), axis=1)
    positions = targets * capacity + ranking

    turned = jnp.swapaxes(chips.reshape(chip_amount, CHIP, CHIP), 1, 2).reshape(chip_amount, -1)
    everyone = lax.all_gather(turned, axes, axis=0, tiled=True)
    own_chips = jnp.take(everyone, targets * chip_amount + target_slot, axis=0)

    slots = jnp.arange(slot_amount, dtype=jnp.int32)
    slot_buffer = jnp.max(
        jnp.where(positions[None, :] == slots[:, None], target_slot[None, :], -1), axis=1
    )
    slots_here = lax.all_to_all(slot_buffer, axes, split_axis=0, concat_axis=0, tiled=True)

    score_buffer = match(
        positions,
        own_chips.reshape(window_amount, CHIP, CHIP),
        windows.reshape(window_amount, WIN, WIN),
        slot_amount,
    )
    scores = lax.all_to_all(score_buffer, axes, split_axis=0, concat_axis=0, tiled=True)
    scores = scores.reshape(slot_amount, CHIP * CHIP)
    hits_table = (slots_here[None, :] == jnp.arange(chip_amount, dtype=jnp.int32)[:, None]).astype(
        jnp.float32
    )
    total = jnp.dot(hits_table, scores, precision=lax.Precision.HIGHEST)
    looks = jnp.sum(hits_table, axis=1)
    average = total / jnp.maximum(looks, 1.0)[:, None]
    grid = average.reshape(-1, GC, CHIP * CHIP)
    extended = padded(grid, ((axes, 0),), 1)
    vertical = extended[:-2] + extended[2:]
    sideways = jnp.pad(grid, ((0, 0), (1, 1), (0, 0)))
    horizontal = sideways[:, :-2] + sideways[:, 2:]
    smoothed = (4.0 * grid + vertical + horizontal) / 8.0
    smoothed = smoothed.reshape(chip_amount, CHIP // 2, 2, CHIP)
    return jnp.swapaxes(smoothed, 1, 2).reshape(1, chip_amount, CHIP * CHIP)


def solution(mesh):
    return jax.shard_map(
        on_device,
        mesh=mesh,
        in_specs=(
            P(("groups", "pair"), ("tile", "sub"), None),
            P(("groups", "pair"), ("tile", "sub"), None),
            P(("groups", "pair"), ("tile", "sub"), None),
            P(("groups", "pair"), ("tile", "sub")),
        ),
        out_specs=P(("groups", "pair"), ("tile", "sub"), None),
        check_vma=False,
    )
```

time: 227 us -> 165 us (0.73)
  matrix products: 98 us -> 2 us
  Pallas kernels: 0 us -> 46.8 us
  between operations: 0.13 us -> 13.5 us
  blocking collectives: 11 us -> 0 us
  other arithmetic: 8.43 us -> 1.42 us
  waiting for transfers between devices: 75.5 us -> 70.9 us
    dot_general x89 -> x1, matrix products: 98 us -> 2 us  [on_device(): total = jnp.dot(hits_table, scores, precision=lax.Precision.HIGHEST)]
    pallas_call x0 -> x1, Pallas kernels: none -> 46.8 us  [match(): pl.pallas_call(match_kernel, out_shape=jax.ShapeDtypeStruct((slot_amount,...]
    all_to_all x3 -> x2, waiting for transfers between devices: 71.7 us -> 46.8 us  [the longest x1 46.8 us: on_device(): lax.all_to_all(score_buffer, axes, split_axis=0, concat_axis=0, tiled=True)]
    all_gather x0 -> x1, waiting for transfers between devices: none -> 22.2 us  [on_device(): everyone = lax.all_gather(turned, axes, axis=0, tiled=True)]
    all_to_all x1 -> x0, blocking collectives: 11 us -> none  [on_device(): lax.all_to_all(requests, ('tile', 'sub'), split_axis=0, concat_axis=0, ti...]
    while x8 -> x0, local copies, waits for them, and re-layouts: 4.69 us -> none
    gather x2, local copies, waits for them, and re-layouts: 2.05 us -> 6.07 us  [on_device(): own_chips = jnp.take(everyone, targets * chip_amount + target_slot, axis=0)]
    scatter x2 -> x0, local copies, waits for them, and re-layouts: 3.51 us -> none  [the longest x1 2.61 us: on_device(): jnp.zeros((slot_amount, offsets * offsets), jnp.float32).at[positions]]
  transfers between devices with their start and end apart: 5 -> 5, of which waited for: 3 -> 4; matrix products, arithmetic and copies ran while one was open for 50% -> 6% of each run, Pallas kernels for 0% -> 28%
where the time goes in v1:
time: 165 us
  waiting for transfers between devices  70.9 us (43%)
  Pallas kernels  46.8 us (28%)
  starting transfers between devices  15.7 us (10%)
  local copies, waits for them, and re-layouts  14.5 us (9%)
  between operations  13.5 us (8%)
  matrix products  2 us (1%)
    all_to_all x1, waiting for transfers between devices, on_device(): lax.all_to_all(score_buffer, axes, split_axis=0, concat_axis=0, tiled=True)  46.8 us
    pallas_call x1, Pallas kernels, match(): pl.pallas_call(match_kernel, out_shape=jax.ShapeDtypeStruct((slot_amount,...  46.8 us
    all_gather x1, waiting for transfers between devices, on_device(): everyone = lax.all_gather(turned, axes, axis=0, tiled=True)  22.2 us
    all_to_all x1, starting transfers between devices, on_device(): lax.all_to_all(slot_buffer, axes, split_axis=0, concat_axis=0, tiled=True)  6.38 us
    gather x2, local copies, waits for them, and re-layouts, on_device(): own_chips = jnp.take(everyone, targets * chip_amount + target_slot, axis=0)  6.07 us
    all_to_all x1, starting transfers between devices, on_device(): lax.all_to_all(score_buffer, axes, split_axis=0, concat_axis=0, tiled=True)  3.78 us
  transfers between devices with their start and end apart: 5, of which 4 were waited for; matrix products, arithmetic and copies ran while one was open for 6% of the time, Pallas kernels for 28%

profile of v1, /device:TPU:1, one launch (start us, length us, event | category | flops | bytes accessed | tf_op | source)
XLA Modules:
  0.0 164.9 jit_solution(5545329335844313512)
XLA Ops:
  6.5 0.0 all-gather.2.cloned.1.call-start
  6.5 1.5 reshape_squeeze.6
  8.0 0.3 copy.11
  8.3 1.2 reshape.79
  9.5 0.0 all-gather.2.cloned.1.call-update
  9.5 0.0 copy-done
  9.5 0.2 convert_reduce_fusion
  9.7 0.1 select_reduce_fusion
  9.8 0.7 all_to_all.9
  10.5 6.4 %all-to-all-start = ((s32[8,16,1]{1,2,0:T(1,128)}), s32[8,16,1]{1,2,0:T(1,128)S(1)}, u32[]{:S(2)}, u32[]{:S(2)}) async-start(s32[8,16,1]{1,2,0:T(1,128)} %bitcast.2), calls=%async_computation | async-start | bytes 8192 | tf_op jit(solution)/shard_map/all_to_all | solution.py:167
  16.9 2.2 %copy.13 = bf16[8,8,128,128]{3,2,1,0:T(8,128)(2,1)S(1)} copy(bf16[8,8,128,128]{3,1,2,0:T(8,128)(2,1)} %bitcast.37) | data formatting | bytes 4194304
  19.1 22.2 %all-gather.2.cloned.1.call-done = bf16[256,4096]{1,0:T(8,128)(2,1)} async-done(((bf16[32,4096]{1,0:T(8,128)(2,1)}), bf16[256,4096]{1,0:T(8,128)(2,1)}) %all-gather.2.cloned.1.call-update) | async-done | bytes 2097168 | tf_op jit(solution)/shard_map/all_gather | solution.py:160
  41.3 4.0 %gather_fusion = bf16[64,4096]{1,0:T(8,128)(2,1)} fusion(bf16[256,4096]{1,0:T(8,128)(2,1)} %all-gather.2.cloned.1.call-done, s32[1024]{0:T(1024)S(1)} %pad_clamp_fusion), kind=kCustom, calls=%fused_computation | custom fusion | bytes 1048832 | tf_op jit(solution)/shard_map/jit(_take)/gather | solution.py:161
  45.3 2.1 %gather.7 = bf16[64,64,64]{2,1,0:T(8,128)(2,1)S(1)} reshape(bf16[64,4096]{1,0:T(8,128)(2,1)} %gather_fusion) | data formatting | bytes 1048576 | tf_op jit(solution)/shard_map/jit(_take)/gather | solution.py:161
  47.3 0.2 broadcast_select_fusion.chips_ref
  47.5 46.8 %shard_map.46 = f32[128,32,128]{2,1,0:T(8,128)} custom-call(s32[64]{0:T(128)S(1)} %multiply_add_fusion.places_ref, bf16[64,64,64]{2,1,0:T(8,128)(2,1)S(1)} %broadcast_select_fusion.chips_ref, bf16[64,128,128]{2,1,0:T(8,128)(2,1)S(1)} %bitcast.33), custom_call_target="tpu_custom_call" | custom-call | flops 8589934592 | bytes 8388608 | tf_op jit(solution)/shard_map/pallas_call | solution.py:119
  94.3 0.0 all-to-all-done
  94.3 3.8 %all-to-all-start.1 = ((f32[128,32,128]{2,1,0:T(8,128)}), f32[128,32,128]{2,1,0:T(8,128)S(1)}, u32[]{:S(2)}, u32[]{:S(2)}) async-start(f32[128,32,128]{2,1,0:T(8,128)} %shard_map.46), calls=%async_computation.1 | async-start | bytes 4194304 | tf_op jit(solution)/shard_map/all_to_all | solution.py:175
  98.1 0.5 broadcast.59
  98.6 0.7 reduce.3
  99.2 0.1 eq.47
  99.3 0.1 convert_reduce_fusion.1
  99.5 46.8 %all-to-all-done.1 = f32[128,32,128]{2,1,0:T(8,128)S(1)} async-done(((f32[128,32,128]{2,1,0:T(8,128)}), f32[128,32,128]{2,1,0:T(8,128)S(1)}, u32[]{:S(2)}, u32[]{:S(2)}) %all-to-all-start.1) | async-done | bytes 2097184 | tf_op jit(solution)/shard_map/all_to_all | solution.py:175
  146.3 2.0 %convolution_divide_fusion = f32[32,4096]{1,0:T(8,128)S(1)} fusion(f32[16,8,32,128]{3,2,1,0:T(8,128)S(1)} %bitcast.34, f32[32]{0:T(128)S(1)} %broadcast_maximum_fusion, s32[128]{0:T(128)S(1)} %eq.47), kind=kOutput, calls=%fused_computation.1 | convolution fusion | flops 201461760 | bytes 2622080 | tf_op jit(solution)/shard_map/dot_general | solution.py:180
  148.3 2.8 %collective-permute-start.1 = (f32[1,8,4096]{2,1,0:T(8,128)S(1)}, f32[1,8,4096]{2,1,0:T(8,128)S(1)}, u32[]{:S(2)}, u32[]{:S(2)}) collective-permute-start(f32[1,8,4096]{2,1,0:T(8,128)S(1)} %get-tuple-element.6), channel_id=1, source_target_pairs={{1,0},{4,1},{5,4},{8,5},{9,8},{12,9},{13,12},{3,2},{6,3},{7,6},{10... | collective-permute-start | bytes 393224 | tf_op jit(solution)/shard_map/ppermute | solution.py:30
  151.1 2.8 %collective-permute-start = (f32[1,8,4096]{2,1,0:T(8,128)S(1)}, f32[1,8,4096]{2,1,0:T(8,128)S(1)}, u32[]{:S(2)}, u32[]{:S(2)}) collective-permute-start(f32[1,8,4096]{2,1,0:T(8,128)S(1)} %get-tuple-element.5), channel_id=1, source_target_pairs={{0,1},{1,4},{4,5},{5,8},{8,9},{9,12},{12,13},{2,3},{3,6},{6,7},{7,... | collective-permute-start | bytes 393224 | tf_op jit(solution)/shard_map/ppermute | solution.py:27
  153.9 0.7 collective-permute-done.1
  154.6 1.2 collective-permute-done
  155.8 0.2 fusion.4
  156.0 0.8 reshape.82
  156.8 0.1 copy.20
  156.9 1.2 reshape.83
  (9 shorter events, 0.1 us)
Async XLA Ops:
  6.5 3.0 %copy-start = (s32[1,64,1]{1,2,0:T(1,128)S(1)}, s32[1,64,1]{1,2,0:T(1,128)}, u32[]{:S(2)}) copy-start(s32[1,64,1]{1,2,0:T(1,128)} %param.6) | copy-start | bytes 772
  6.5 3.2 %copy-start.1 = (s32[1,64]{1,0:T(1,128)S(1)}, s32[1,64]{1,0:T(1,128)}, u32[]{:S(2)}) copy-start(s32[1,64]{1,0:T(1,128)} %param.7) | copy-start | bytes 772
  6.5 34.7 %all-gather.2.cloned.1.call-start = ((), (), s32[]{:S(2)}) async-start(), calls=%async_computation.2 | async-start | bytes 2359296 | tf_op jit(solution)/shard_map/all_gather | solution.py:160
  10.5 83.8 %all-to-all-start = ((s32[8,16,1]{1,2,0:T(1,128)}), s32[8,16,1]{1,2,0:T(1,128)S(1)}, u32[]{:S(2)}, u32[]{:S(2)}) async-start(s32[8,16,1]{1,2,0:T(1,128)} %bitcast.2), calls=%async_computation | async-start | bytes 8192 | tf_op jit(solution)/shard_map/all_to_all | solution.py:167
  94.3 52.0 %all-to-all-start.1 = ((f32[128,32,128]{2,1,0:T(8,128)}), f32[128,32,128]{2,1,0:T(8,128)S(1)}, u32[]{:S(2)}, u32[]{:S(2)}) async-start(f32[128,32,128]{2,1,0:T(8,128)} %shard_map.46), calls=%async_computation.1 | async-start | bytes 4194304 | tf_op jit(solution)/shard_map/all_to_all | solution.py:175
  148.3 6.3 %collective-permute-start.1 = (f32[1,8,4096]{2,1,0:T(8,128)S(1)}, f32[1,8,4096]{2,1,0:T(8,128)S(1)}, u32[]{:S(2)}, u32[]{:S(2)}) collective-permute-start(f32[1,8,4096]{2,1,0:T(8,128)S(1)} %get-tuple-element.6), channel_id=1, source_target_pairs={{1,0},{4,1},{5,4},{8,5},{9,8},{12,9},{13,12},{3,2},{6,3},{7,6},{10... | collective-permute-start | bytes 393224 | tf_op jit(solution)/shard_map/ppermute | solution.py:30
  151.1 4.7 %collective-permute-start = (f32[1,8,4096]{2,1,0:T(8,128)S(1)}, f32[1,8,4096]{2,1,0:T(8,128)S(1)}, u32[]{:S(2)}, u32[]{:S(2)}) collective-permute-start(f32[1,8,4096]{2,1,0:T(8,128)S(1)} %get-tuple-element.5), channel_id=1, source_target_pairs={{0,1},{1,4},{4,5},{5,8},{8,9},{9,12},{12,13},{2,3},{3,6},{6,7},{7,... | collective-permute-start | bytes 393224 | tf_op jit(solution)/shard_map/ppermute | solution.py:27
Sparse Core Ops, SparseCore 0:
  9.6 31.5 all-gather.1

commit v2 on v1

v2 whole, which is shorter than its diff:
```python
import functools

import jax
import jax.numpy as jnp
from jax import lax
from jax.experimental import pallas as pl
from jax.experimental.pallas import tpu as pltpu
from jax.sharding import PartitionSpec as P

CHIP = 64
WIN = 128
GC = 8
LANES = 128
SUBLANES = 8
PHASES = 4
DEPTH = 80
EACH = 2

epsilon = 1e-06


def padded(block, sides, width):
    for axis, dim in sides:
        count = lax.axis_size(axis)
        forward = [(i, i + 1) for i in range(count - 1)]
        backward = [(target, source) for source, target in forward]
        low = lax.ppermute(
            lax.slice_in_dim(block, block.shape[dim] - width, None, axis=dim), axis, forward
        )
        high = lax.ppermute(lax.slice_in_dim(block, 0, width, axis=dim), axis, backward)
        block = jnp.concatenate([low, block, high], axis=dim)
    return block


def box_sums(image):
    step = 1
    while step < CHIP:
        image = image + pltpu.roll(image, WIN - step, 0)
        step *= 2
    image = image[:CHIP]
    step = 1
    while step < CHIP:
        image = image + pltpu.roll(image, WIN - step, 1)
        step *= 2
    return image


def patch_kernel(windows_ref, first_ref, inverse_ref):
    for item in range(windows_ref.shape[0]):
        window = windows_ref[item].astype(jnp.float32)
        first = box_sums(window)
        second = box_sums(window * window)
        patch_mean = first / (CHIP * CHIP)
        patch_var = second / (CHIP * CHIP) - patch_mean * patch_mean
        first_ref[item] = first
        inverse_ref[item] = 1.0 / (CHIP * jnp.sqrt(patch_var + epsilon))


def patches(windows):
    amount = windows.shape[0]
    surface = jax.ShapeDtypeStruct((amount, CHIP, LANES), jnp.float32)
    block = pl.BlockSpec((EACH, CHIP, LANES), lambda i: (i, 0, 0))
    return pl.pallas_call(
        patch_kernel,
        out_shape=(surface, surface),
        grid=(amount // EACH,),
        in_specs=[pl.BlockSpec((EACH, WIN, WIN), lambda i: (i, 0, 0))],
        out_specs=(block, block),
        cost_estimate=pl.CostEstimate(
            flops=amount * 2 * 128 * 512 * 256, bytes_accessed=40 * 1024 * 1024, transcendentals=0
        ),
    )(windows)


def correlate(chip_ref, window_ref, first_ref, inverse_ref, even_ref, odd_ref):
    half = CHIP // 2
    chip = chip_ref[...].astype(jnp.float32)
    total = jnp.sum(jnp.sum(chip, axis=0, keepdims=True), axis=1, keepdims=True)
    mean = total / (CHIP * CHIP)
    centred = chip - mean
    square = jnp.sum(jnp.sum(centred * centred, axis=0, keepdims=True), axis=1, keepdims=True)
    chip_std = jnp.sqrt(square / (CHIP * CHIP) + epsilon)

    lane = lax.broadcasted_iota(jnp.int32, (half, LANES), 1)
    wide = (jnp.where(lane < CHIP, chip, 0.0), jnp.where(lane < CHIP, pltpu.roll(chip, CHIP, 1), 0.0))
    left = []
    for phase in range(PHASES):
        rows = []
        for v in range(phase, CHIP, PHASES):
            row = wide[v // half][v % half : v % half + 1]
            row = jnp.broadcast_to(row, (SUBLANES, LANES))
            rows.append(pltpu.roll(row, 0, 1, stride=1, stride_axis=0))
        left.append(jnp.concatenate(rows, axis=0).astype(jnp.bfloat16)[:, :DEPTH])
    left = jnp.concatenate(left, axis=1)

    window = window_ref[...].astype(jnp.float32)
    for phase in range(PHASES):
        moved = window if phase == 0 else pltpu.roll(window, WIN - phase, 1)
        even_ref[phase] = moved.astype(jnp.bfloat16)
        odd_ref[phase] = pltpu.roll(moved, WIN - SUBLANES, 0).astype(jnp.bfloat16)

    groups = CHIP // SUBLANES
    surfaces = []
    for pair in range(groups // 2):
        start = 2 * SUBLANES * pair
        right = jnp.concatenate(
            [
                jnp.concatenate([ref[phase, start : start + DEPTH] for phase in range(PHASES)], axis=0)
                for ref in (even_ref, odd_ref)
            ],
            axis=1,
        )
        partial = jnp.dot(left, right, preferred_element_type=jnp.float32)
        for side in range(2):
            part = partial[:, side * LANES : (side + 1) * LANES]
            value = part[:SUBLANES]
            for far in range(1, CHIP // PHASES):
                rows = part[far * SUBLANES : (far + 1) * SUBLANES]
                value = value + pltpu.roll(rows, LANES - PHASES * far, 1)
            surfaces.append(value)
    raw = jnp.concatenate(surfaces, axis=0)
    return (raw - mean * first_ref[...]) * (inverse_ref[...] / chip_std)


def match_kernel(places_ref, names_ref, *refs):
    chips, rest = refs[:EACH], refs[EACH:]
    windows_ref, first_ref, inverse_ref, out_ref, scale_ref, even_ref, odd_ref = rest
    step = pl.program_id(0)

    @pl.when(step == 0)
    def _():
        out_ref[...] = jnp.zeros_like(out_ref)
        scale_ref[...] = jnp.zeros_like(scale_ref)

    half = CHIP // 2
    lane = lax.broadcasted_iota(jnp.int32, (half, LANES), 1)
    for item in range(EACH):
        score = correlate(
            chips[item].at[0],
            windows_ref.at[item],
            first_ref.at[item],
            inverse_ref.at[item],
            even_ref.at[item],
            odd_ref.at[item],
        )
        low, high = score[:half], pltpu.roll(score[half:], CHIP, 1)
        packed = jnp.where(lane < CHIP, low, high)
        size = jnp.abs(packed)
        largest = jnp.max(jnp.max(size, axis=0, keepdims=True), axis=1, keepdims=True)
        largest = jnp.maximum(largest, 1e-30)
        code = jnp.sqrt(size * (1.0 / largest)) * 32767.0
        code = jnp.minimum(code + 0.5, 32767.0).astype(jnp.int32)
        code = jnp.where(packed < 0, -code, code)
        place = places_ref[step * EACH + item]
        out_ref[place] = code.astype(jnp.int16)
        scale_ref[place] = jnp.broadcast_to(largest, (SUBLANES, LANES))


def match(positions, names, everyone, windows, first, inverse, slot_amount):
    amount = windows.shape[0]
    half = CHIP // 2

    def chip_spec(item):
        return pl.BlockSpec((1, half, LANES), lambda i, p, n: (n[i * EACH + item], 0, 0))

    surface = pl.BlockSpec((EACH, CHIP, LANES), lambda i, p, n: (i, 0, 0))
    return pl.pallas_call(
        match_kernel,
        out_shape=(
            jax.ShapeDtypeStruct((slot_amount, half, LANES), jnp.int16),
            jax.ShapeDtypeStruct((slot_amount, SUBLANES, LANES), jnp.float32),
        ),
        grid_spec=pltpu.PrefetchScalarGridSpec(
            num_scalar_prefetch=2,
            grid=(amount // EACH,),
            in_specs=[chip_spec(item) for item in range(EACH)]
            + [pl.BlockSpec((EACH, WIN, WIN), lambda i, p, n: (i, 0, 0)), surface, surface],
            out_specs=(
                pl.BlockSpec((slot_amount, half, LANES), lambda i, p, n: (0, 0, 0)),
                pl.BlockSpec((slot_amount, SUBLANES, LANES), lambda i, p, n: (0, 0, 0)),
            ),
            scratch_shapes=[
                pltpu.VMEM((EACH, PHASES, WIN, LANES), jnp.bfloat16),
                pltpu.VMEM((EACH, PHASES, WIN, LANES), jnp.bfloat16),
            ],
        ),
        compiler_params=pltpu.CompilerParams(vmem_limit_bytes=40 * 1024 * 1024),
        cost_estimate=pl.CostEstimate(
            flops=amount * 2 * 128 * 512 * 1024, bytes_accessed=8 * 1024 * 1024, transcendentals=0
        ),
    )(positions, names, *([everyone] * EACH), windows, first, inverse)


def on_device(ref_chips, search_windows, dest_block, dest_slot):
    axes = ("tile", "sub")
    chips = ref_chips[0]
    windows = search_windows[0]
    targets = dest_block[0, :, 0]
    target_slot = dest_slot[0]
    window_amount = windows.shape[0]
    chip_amount = chips.shape[0]
    half = CHIP // 2
    devices = lax.axis_size(axes)
    capacity = max(2, 2 * window_amount // devices)
    slot_amount = devices * capacity

    turned = jnp.swapaxes(chips.reshape(chip_amount, CHIP, CHIP), 1, 2)
    turned = jnp.swapaxes(turned.reshape(chip_amount, 2, half, CHIP), 1, 2)
    everyone = lax.all_gather(turned.reshape(chip_amount, half, LANES), axes, axis=0, tiled=True)

    order = jnp.arange(window_amount, dtype=jnp.int32)
    matches = targets[:, None] == targets[None, :]
    earlier = order[:, None] > order[None, :]
    ranking = jnp.sum((matches & earlier).astype(jnp.int32), axis=1)
    positions = targets * capacity + ranking
    slots = jnp.arange(slot_amount, dtype=jnp.int32)
    slot_buffer = jnp.max(
        jnp.where(positions[None, :] == slots[:, None], target_slot[None, :], -1), axis=1
    )

    windows = windows.reshape(window_amount, WIN, WIN)
    first, inverse = patches(windows)
    codes, scales = match(
        positions,
        targets * chip_amount + target_slot,
        everyone,
        windows,
        first,
        inverse,
        slot_amount,
    )
    codes = lax.all_to_all(codes, axes, split_axis=0, concat_axis=0, tiled=True)
    notes = jnp.concatenate([scales[:, 0, 0], slot_buffer.astype(jnp.float32)])
    notes = lax.all_gather(notes, axes, axis=0).reshape(devices, 2, devices, capacity)
    notes = lax.dynamic_index_in_dim(notes, lax.axis_index(axes), 2, keepdims=False)
    notes = notes.transpose(0, 2, 1).reshape(slot_amount, 2)
    codes = codes.astype(jnp.float32) * (1.0 / 32767.0)
    scores = (codes * jnp.abs(codes)).reshape(slot_amount, CHIP * CHIP)
    hits_table = (
        notes[None, :, 1] == jnp.arange(chip_amount, dtype=jnp.float32)[:, None]
    ).astype(jnp.float32)
    looks = jnp.sum(hits_table, axis=1)
    share = hits_table * notes[None, :, 0] / jnp.maximum(looks, 1.0)[:, None]
    average = jnp.dot(share, scores, precision=lax.Precision.HIGHEST)
    grid = average.reshape(-1, GC, CHIP * CHIP)
    extended = padded(grid, ((axes, 0),), 1)
    vertical = extended[:-2] + extended[2:]
    sideways = jnp.pad(grid, ((0, 0), (1, 1), (0, 0)))
    horizontal = sideways[:, :-2] + sideways[:, 2:]
    smoothed = (4.0 * grid + vertical + horizontal) / 8.0
    smoothed = smoothed.reshape(chip_amount, half, 2, CHIP)
    return jnp.swapaxes(smoothed, 1, 2).reshape(1, chip_amount, CHIP * CHIP)


def solution(mesh):
    return jax.shard_map(
        on_device,
        mesh=mesh,
        in_specs=(
            P(("groups", "pair"), ("tile", "sub"), None),
            P(("groups", "pair"), ("tile", "sub"), None),
            P(("groups", "pair"), ("tile", "sub"), None),
            P(("groups", "pair"), ("tile", "sub")),
        ),
        out_specs=P(("groups", "pair"), ("tile", "sub"), None),
        check_vma=False,
    )
```

time: 165 us -> 135 us (0.82)
  the two profiles are of different devices: /device:TPU:1 before, /device:TPU:30 now
where the time goes in v2:
time: 135 us; the launch traced here: 133 us
  Pallas kernels  58.3 us (43%)
  blocking collectives  25.8 us (19%)
  between operations  13.6 us (10%)
  local copies, waits for them, and re-layouts  13.3 us (10%)
  starting transfers between devices  11.4 us (8%)
  waiting for transfers between devices  7.5 us (6%)
  matrix products  2.32 us (2%)
    pallas_call x1, Pallas kernels, match(): pl.pallas_call(match_kernel, out_shape=(jax.ShapeDtypeStruct((slot_amount...  34.2 us
    all_gather x1, blocking collectives, on_device(): lax.all_gather(notes, axes, axis=0).reshape(devices, 2, devices, capacity)  25.8 us
    pallas_call x1, Pallas kernels, patches(): pl.pallas_call(patch_kernel, out_shape=(surface, surface), grid=(amount /...  24.1 us
    unnamed x15, local copies, waits for them, and re-layouts  6.71 us
    all_to_all x1, starting transfers between devices, on_device(): codes = lax.all_to_all(codes, axes, split_axis=0, concat_axis=0, tiled=True)  5.92 us
    ppermute x1, waiting for transfers between devices, padded(): lax.ppermute(lax.slice_in_dim(block, block.shape[dim] - width, None, axis...  3.79 us
    ppermute x1, starting transfers between devices, padded(): lax.ppermute(lax.slice_in_dim(block, 0, width, axis=dim), axis, backward)  3.54 us
    all_gather x1, waiting for transfers between devices, on_device(): lax.all_gather(turned.reshape(chip_amount, half, LANES), axes, axis=0, ti...  3.12 us
  transfers between devices with their start and end apart: 4, of which 3 were waited for; matrix products, arithmetic and copies ran while one was open for 3% of the time, Pallas kernels for 18%

profile of v2, /device:TPU:30, one launch (start us, length us, event | category | flops | bytes accessed | tf_op | source)
XLA Modules:
  0.0 133.3 jit_solution(12160276000659599799)
XLA Ops:
  6.5 1.6 %reshape_squeeze.6 = bf16[32,64,64]{2,1,0:T(8,128)(2,1)S(1)} reshape(bf16[1,32,4096]{2,1,0:T(8,128)(2,1)} %param.4) | data formatting | bytes 524288 | tf_op jit(solution)/shard_map/reshape;squeeze | solution.py:207
  8.2 0.3 copy.19
  8.4 0.5 copy.20
  9.0 1.0 reshape.42
  9.9 0.0 all-gather.4.cloned.1.call-update
  10.0 0.0 copy-start.5
  10.0 1.9 %copy.23 = bf16[8,8,128,128]{3,2,1,0:T(8,128)(2,1)} copy(bf16[8,8,128,128]{3,1,2,0:T(8,128)(2,1)S(1)} %bitcast.43) | data formatting | bytes 4194304
  11.9 0.2 convert_reduce_fusion
  12.1 0.0 copy-start.6
  12.1 24.1 %shard_map.46 = (f32[64,64,128]{2,1,0:T(8,128)}, f32[64,64,128]{2,1,0:T(8,128)}) custom-call(bf16[64,128,128]{2,1,0:T(8,128)(2,1)} %bitcast.38), custom_call_target="tpu_custom_call" | custom-call | flops 2147483648 | bytes 41943040 | tf_op jit(solution)/shard_map/pallas_call | solution.py:63
  36.2 3.1 %all-gather.4.cloned.1.call-done.refs_0_.refs_1_ = bf16[256,32,128]{2,1,0:T(8,128)(2,1)} async-done(((bf16[32,32,128]{2,1,0:T(8,128)(2,1)}), bf16[256,32,128]{2,1,0:T(8,128)(2,1)}) %all-gather.4.cloned.1.call-update) | async-done | bytes 2097168 | tf_op jit(solution)/shard_map/all_gather | solution.py:209
  39.3 1.6 %copy-done.1 = bf16[256,32,128]{2,1,0:T(8,128)(2,1)S(1)} copy-done((bf16[256,32,128]{2,1,0:T(8,128)(2,1)S(1)}, bf16[256,32,128]{2,1,0:T(8,128)(2,1)}, u32[]{:S(2)}) %copy-start.1) | copy-done | bytes 2097176
  40.9 1.6 %copy-done.2 = f32[64,64,128]{2,1,0:T(8,128)S(1)} copy-done((f32[64,64,128]{2,1,0:T(8,128)S(1)}, f32[64,64,128]{2,1,0:T(8,128)}, u32[]{:S(2)}) %copy-start.2) | copy-done | bytes 2097176
  42.5 1.6 %copy-done.3 = f32[64,64,128]{2,1,0:T(8,128)S(1)} copy-done((f32[64,64,128]{2,1,0:T(8,128)S(1)}, f32[64,64,128]{2,1,0:T(8,128)}, u32[]{:S(2)}) %copy-start.3) | copy-done | bytes 2097176
  44.1 34.2 %shard_map.47 = (s16[128,32,128]{2,1,0:T(8,128)(2,1)}, f32[128,8,128]{2,1,0:T(8,128)S(1)}) custom-call(s32[64]{0:T(128)S(1)} %get-tuple-element.18.places_ref, s32[64]{0:T(128)S(1)} %get-tuple-element.17.names_ref, bf16[256,32,128]{2,1,0:T(8,128)(2,1)S(1)} %copy-done.1, bf16[256,32,128]{2,1,0:T(8,128)(2,1)S(1)} %copy-done.1, ...), custom_call_target="tpu_custom_call" | custom-call | flops 8589934592 | bytes 8388608 | tf_op jit(solution)/shard_map/pallas_call | solution.py:167
  78.3 5.9 %all-to-all-start = ((s16[128,32,128]{2,1,0:T(8,128)(2,1)}), s16[128,32,128]{2,1,0:T(8,128)(2,1)S(1)}, u32[]{:S(2)}, u32[]{:S(2)}) async-start(s16[128,32,128]{2,1,0:T(8,128)(2,1)} %get-tuple-element.12), calls=%async_computation | async-start | bytes 2097152 | tf_op jit(solution)/shard_map/all_to_all | solution.py:232
  84.2 0.1 select_reduce_fusion
  84.3 1.0 slice_reduce_fusion
  85.4 25.8 %all-gather.1 = f32[8,1,256]{2,1,0:T(1,128)S(1)} all-gather(f32[1,1,256]{2,1,0:T(1,128)S(1)} %bitcast.47), channel_id=2, replica_groups=mesh['groups'=2,'tile'=4,'pair'=2,'sub'=2] {'tile','sub'}, dimensions={0}, use_global_device_ids=true | all-gather | bytes 9216 | tf_op jit(solution)/shard_map/all_gather | solution.py:234
  111.2 0.1 reshape.43
  111.3 0.1 reshape.44
  111.4 0.1 convert_reduce_fusion.1
  111.5 0.5 abs_multiply_fusion
  112.0 2.3 %fusion = f32[32,4096]{1,0:T(8,128)S(1)} fusion(f32[16,8,32,128]{3,2,1,0:T(8,128)S(1)} %bitcast.40, f32[32]{0:T(128)S(1)} %broadcast_maximum_fusion, f32[128]{0:T(128)S(1)} %get-tuple-element.15, f32[128]{0:T(128)S(1)} %get-tuple-element.16), kind=kOutput, calls=%fused_computation.1 | convolution fusion | flops 201338880 | bytes 2622592 | tf_op jit(solution)/shard_map/dot_general | solution.py:244
  114.4 3.5 %collective-permute-start.1 = (f32[1,8,4096]{2,1,0:T(8,128)S(1)}, f32[1,8,4096]{2,1,0:T(8,128)S(1)}, u32[]{:S(2)}, u32[]{:S(2)}) collective-permute-start(f32[1,8,4096]{2,1,0:T(8,128)S(1)} %get-tuple-element.14), channel_id=1, source_target_pairs={{1,0},{4,1},{5,4},{8,5},{9,8},{12,9},{13,12},{3,2},{6,3},{7,6},{10... | collective-permute-start | bytes 393224 | tf_op jit(solution)/shard_map/ppermute | solution.py:30
  117.9 1.9 %collective-permute-start = (f32[1,8,4096]{2,1,0:T(8,128)S(1)}, f32[1,8,4096]{2,1,0:T(8,128)S(1)}, u32[]{:S(2)}, u32[]{:S(2)}) collective-permute-start(f32[1,8,4096]{2,1,0:T(8,128)S(1)} %get-tuple-element.13), channel_id=1, source_target_pairs={{0,1},{1,4},{4,5},{5,8},{8,9},{9,12},{12,13},{2,3},{3,6},{6,7},{7,... | collective-permute-start | bytes 393224 | tf_op jit(solution)/shard_map/ppermute | solution.py:27
  119.9 0.6 collective-permute-done.1
  120.4 3.8 %collective-permute-done = f32[1,8,4096]{2,1,0:T(8,128)S(1)} collective-permute-done((f32[1,8,4096]{2,1,0:T(8,128)S(1)}, f32[1,8,4096]{2,1,0:T(8,128)S(1)}, u32[]{:S(2)}, u32[]{:S(2)}) %collective-permute-start) | collective-permute-done | bytes 131104 | tf_op jit(solution)/shard_map/ppermute | solution.py:27
  124.2 0.2 fusion.5
  124.4 0.8 reshape.47
  125.2 0.1 copy.31
  125.3 1.2 reshape.48
  (20 shorter events, 0.1 us)
Async XLA Ops:
  6.5 3.4 %copy-start.4 = (bf16[1,64,16384]{2,1,0:T(8,128)(2,1)S(1)}, bf16[1,64,16384]{2,1,0:T(8,128)(2,1)}, u32[]{:S(2)}) copy-start(bf16[1,64,16384]{2,1,0:T(8,128)(2,1)} %param.5) | copy-start | bytes 6291460
  6.5 32.8 %all-gather.4.cloned.1.call-start = ((), (), s32[]{:S(2)}) async-start(), calls=%async_computation.1 | async-start | bytes 2359296 | tf_op jit(solution)/shard_map/all_gather | solution.py:209
  10.0 1.9 %copy-start.5 = (s32[1,64,1]{1,2,0:T(1,128)S(1)}, s32[1,64,1]{1,2,0:T(1,128)}, u32[]{:S(2)}) copy-start(s32[1,64,1]{1,2,0:T(1,128)} %param.6) | copy-start | bytes 772
  12.1 24.1 %copy-start.6 = (s32[1,64]{1,0:T(1,128)S(1)}, s32[1,64]{1,0:T(1,128)}, u32[]{:S(2)}) copy-start(s32[1,64]{1,0:T(1,128)} %param.7) | copy-start | bytes 772
  12.1 27.2 %copy-start = (bf16[8,8,128,128]{3,2,1,0:T(8,128)(2,1)S(1)}, bf16[8,8,128,128]{3,2,1,0:T(8,128)(2,1)}, u32[]{:S(2)}) copy-start(bf16[8,8,128,128]{3,2,1,0:T(8,128)(2,1)} %copy.23) | copy-start | bytes 6291460
  39.3 1.6 %copy-start.1 = (bf16[256,32,128]{2,1,0:T(8,128)(2,1)S(1)}, bf16[256,32,128]{2,1,0:T(8,128)(2,1)}, u32[]{:S(2)}) copy-start(bf16[256,32,128]{2,1,0:T(8,128)(2,1)} %all-gather.4.cloned.1.call-done.refs_0_.refs_1_) | copy-start | bytes 6291460
  40.9 1.6 %copy-start.2 = (f32[64,64,128]{2,1,0:T(8,128)S(1)}, f32[64,64,128]{2,1,0:T(8,128)}, u32[]{:S(2)}) copy-start(f32[64,64,128]{2,1,0:T(8,128)} %get-tuple-element.9.refs_3_) | copy-start | bytes 6291460
  42.5 1.6 %copy-start.3 = (f32[64,64,128]{2,1,0:T(8,128)S(1)}, f32[64,64,128]{2,1,0:T(8,128)}, u32[]{:S(2)}) copy-start(f32[64,64,128]{2,1,0:T(8,128)} %get-tuple-element.10.refs_4_) | copy-start | bytes 6291460
  78.3 33.3 %all-to-all-start = ((s16[128,32,128]{2,1,0:T(8,128)(2,1)}), s16[128,32,128]{2,1,0:T(8,128)(2,1)S(1)}, u32[]{:S(2)}, u32[]{:S(2)}) async-start(s16[128,32,128]{2,1,0:T(8,128)(2,1)} %get-tuple-element.12), calls=%async_computation | async-start | bytes 2097152 | tf_op jit(solution)/shard_map/all_to_all | solution.py:232
  114.4 6.0 %collective-permute-start.1 = (f32[1,8,4096]{2,1,0:T(8,128)S(1)}, f32[1,8,4096]{2,1,0:T(8,128)S(1)}, u32[]{:S(2)}, u32[]{:S(2)}) collective-permute-start(f32[1,8,4096]{2,1,0:T(8,128)S(1)} %get-tuple-element.14), channel_id=1, source_target_pairs={{1,0},{4,1},{5,4},{8,5},{9,8},{12,9},{13,12},{3,2},{6,3},{7,6},{10... | collective-permute-start | bytes 393224 | tf_op jit(solution)/shard_map/ppermute | solution.py:30
  117.9 6.3 %collective-permute-start = (f32[1,8,4096]{2,1,0:T(8,128)S(1)}, f32[1,8,4096]{2,1,0:T(8,128)S(1)}, u32[]{:S(2)}, u32[]{:S(2)}) collective-permute-start(f32[1,8,4096]{2,1,0:T(8,128)S(1)} %get-tuple-element.13), channel_id=1, source_target_pairs={{0,1},{1,4},{4,5},{5,8},{8,9},{9,12},{12,13},{2,3},{3,6},{6,7},{7,... | collective-permute-start | bytes 393224 | tf_op jit(solution)/shard_map/ppermute | solution.py:27
Sparse Core Ops, SparseCore 0:
  10.1 29.2 all-gather.3

commit v3 on v2

--- a/solution.py
+++ b/solution.py
@@ -13,8 +13,9 @@
 LANES = 128
 SUBLANES = 8
 PHASES = 4
-DEPTH = 80
-EACH = 2
+GROUP = 16
+DEPTH = CHIP + GROUP
+EACH = 4
 
 epsilon = 1e-06
 
@@ -72,7 +73,7 @@
     )(windows)
 
 
-def correlate(chip_ref, window_ref, first_ref, inverse_ref, even_ref, odd_ref):
+def correlate(chip_ref, window_ref, first_ref, inverse_ref, copies_ref):
     half = CHIP // 2
     chip = chip_ref[...].astype(jnp.float32)
     total = jnp.sum(jnp.sum(chip, axis=0, keepdims=True), axis=1, keepdims=True)
@@ -89,33 +90,35 @@
         for v in range(phase, CHIP, PHASES):
             row = wide[v // half][v % half : v % half + 1]
             row = jnp.broadcast_to(row, (SUBLANES, LANES))
-            rows.append(pltpu.roll(row, 0, 1, stride=1, stride_axis=0))
+            row = pltpu.roll(row, 0, 1, stride=1, stride_axis=0)
+            rows += [row, pltpu.roll(row, SUBLANES, 1)]
         left.append(jnp.concatenate(rows, axis=0).astype(jnp.bfloat16)[:, :DEPTH])
     left = jnp.concatenate(left, axis=1)
 
     window = window_ref[...].astype(jnp.float32)
     for phase in range(PHASES):
         moved = window if phase == 0 else pltpu.roll(window, WIN - phase, 1)
-        even_ref[phase] = moved.astype(jnp.bfloat16)
-        odd_ref[phase] = pltpu.roll(moved, WIN - SUBLANES, 0).astype(jnp.bfloat16)
-
-    groups = CHIP // SUBLANES
+        copies_ref[phase] = moved.astype(jnp.bfloat16)
+
+    groups = CHIP // GROUP
     surfaces = []
     for pair in range(groups // 2):
-        start = 2 * SUBLANES * pair
+        starts = (2 * GROUP * pair, 2 * GROUP * pair + GROUP)
         right = jnp.concatenate(
             [
-                jnp.concatenate([ref[phase, start : start + DEPTH] for phase in range(PHASES)], axis=0)
-                for ref in (even_ref, odd_ref)
+                jnp.concatenate(
+                    [copies_ref[phase, start : start + DEPTH] for phase in range(PHASES)], axis=0
+                )
+                for start in starts
             ],
             axis=1,
         )
         partial = jnp.dot(left, right, preferred_element_type=jnp.float32)
         for side in range(2):
             part = partial[:, side * LANES : (side + 1) * LANES]
-            value = part[:SUBLANES]
+            value = part[:GROUP]
             for far in range(1, CHIP // PHASES):
-                rows = part[far * SUBLANES : (far + 1) * SUBLANES]
+                rows = part[far * GROUP : (far + 1) * GROUP]
                 value = value + pltpu.roll(rows, LANES - PHASES * far, 1)
             surfaces.append(value)
     raw = jnp.concatenate(surfaces, axis=0)
@@ -124,7 +127,7 @@
 
 def match_kernel(places_ref, names_ref, *refs):
     chips, rest = refs[:EACH], refs[EACH:]
-    windows_ref, first_ref, inverse_ref, out_ref, scale_ref, even_ref, odd_ref = rest
+    windows_ref, first_ref, inverse_ref, out_ref, scale_ref, copies_ref = rest
     step = pl.program_id(0)
 
     @pl.when(step == 0)
@@ -140,8 +143,7 @@
             windows_ref.at[item],
             first_ref.at[item],
             inverse_ref.at[item],
-            even_ref.at[item],
-            odd_ref.at[item],
+            copies_ref.at[item],
         )
         low, high = score[:half], pltpu.roll(score[half:], CHIP, 1)
         packed = jnp.where(lane < CHIP, low, high)
@@ -181,10 +183,9 @@
             ),
             scratch_shapes=[
                 pltpu.VMEM((EACH, PHASES, WIN, LANES), jnp.bfloat16),
-                pltpu.VMEM((EACH, PHASES, WIN, LANES), jnp.bfloat16),
             ],
         ),
-        compiler_params=pltpu.CompilerParams(vmem_limit_bytes=40 * 1024 * 1024),
+        compiler_params=pltpu.CompilerParams(vmem_limit_bytes=58 * 1024 * 1024),
         cost_estimate=pl.CostEstimate(
             flops=amount * 2 * 128 * 512 * 1024, bytes_accessed=8 * 1024 * 1024, transcendentals=0
         ),

time: 135 us -> 140 us (1.037)
  the two profiles are of different devices: /device:TPU:30 before, /device:TPU:1 now
where the time goes in v3:
time: 140 us; the launch traced here: 139 us
  Pallas kernels  61.7 us (44%)
  blocking collectives  22.4 us (16%)
  waiting for transfers between devices  16.8 us (12%)
  between operations  13.5 us (10%)
  starting transfers between devices  10.8 us (8%)
  local copies, waits for them, and re-layouts  9.58 us (7%)
  matrix products  2.32 us (2%)
  other arithmetic  1.67 us (1%)
    pallas_call x1, Pallas kernels, match(): pl.pallas_call(match_kernel, out_shape=(jax.ShapeDtypeStruct((slot_amount...  46.6 us
    all_gather x1, blocking collectives, on_device(): lax.all_gather(notes, axes, axis=0).reshape(devices, 2, devices, capacity)  22.4 us
    pallas_call x1, Pallas kernels, patches(): pl.pallas_call(patch_kernel, out_shape=(surface, surface), grid=(amount /...  15.1 us
    all_gather x1, waiting for transfers between devices, on_device(): lax.all_gather(turned.reshape(chip_amount, half, LANES), axes, axis=0, ti...  14 us
    ppermute x1, starting transfers between devices, padded(): lax.ppermute(lax.slice_in_dim(block, block.shape[dim] - width, None, axis...  4.25 us
    all_to_all x1, starting transfers between devices, on_device(): codes = lax.all_to_all(codes, axes, split_axis=0, concat_axis=0, tiled=True)  3.73 us
  transfers between devices with their start and end apart: 4, of which 4 were waited for; matrix products, arithmetic and copies ran while one was open for 4% of the time, Pallas kernels for 11%

profile of v3, /device:TPU:1, one launch (start us, length us, event | category | flops | bytes accessed | tf_op | source)
XLA Modules:
  0.0 138.7 jit_solution(13787545027161965773)
XLA Ops:
  6.5 0.0 all-gather.4.cloned.1.call-start
  6.5 1.6 %reshape_squeeze.6 = bf16[32,64,64]{2,1,0:T(8,128)(2,1)S(1)} reshape(bf16[1,32,4096]{2,1,0:T(8,128)(2,1)} %param.4) | data formatting | bytes 524288 | tf_op jit(solution)/shard_map/reshape;squeeze | solution.py:208
  8.2 0.3 copy.19
  8.4 0.5 copy.20
  9.0 1.0 reshape.42
  9.9 0.0 all-gather.4.cloned.1.call-update
  10.0 0.0 copy-start.1
  10.0 1.9 %copy.23 = bf16[8,8,128,128]{3,2,1,0:T(8,128)(2,1)} copy(bf16[8,8,128,128]{3,1,2,0:T(8,128)(2,1)S(1)} %bitcast.41) | data formatting | bytes 4194304
  11.9 0.2 convert_reduce_fusion
  12.0 0.0 copy-start.2
  12.0 15.1 %shard_map.46 = (f32[64,64,128]{2,1,0:T(8,128)}, f32[64,64,128]{2,1,0:T(8,128)}) custom-call(bf16[64,128,128]{2,1,0:T(8,128)(2,1)} %bitcast.42), custom_call_target="tpu_custom_call" | custom-call | flops 2147483648 | bytes 41943040 | tf_op jit(solution)/shard_map/pallas_call | solution.py:64
  27.1 0.6 multiply_add_fusion
  27.7 14.0 %all-gather.4.cloned.1.call-done.refs_0_.refs_1_.refs_2_.refs_3_ = bf16[256,32,128]{2,1,0:T(8,128)(2,1)} async-done(((bf16[32,32,128]{2,1,0:T(8,128)(2,1)}), bf16[256,32,128]{2,1,0:T(8,128)(2,1)}) %all-gather.4.cloned.1.call-update) | async-done | bytes 2097168 | tf_op jit(solution)/shard_map/all_gather | solution.py:210
  41.7 46.6 %shard_map.47 = (s16[128,32,128]{2,1,0:T(8,128)(2,1)}, f32[128,8,128]{2,1,0:T(8,128)}) custom-call(s32[64]{0:T(128)} %get-tuple-element.18.places_ref, s32[64]{0:T(128)} %get-tuple-element.17.names_ref, bf16[256,32,128]{2,1,0:T(8,128)(2,1)} %all-gather.4.cloned.1.call-done.refs_0_.refs_1_.refs_2_.refs_3_, ...), custom_call_target="tpu_custom_call" | custom-call | flops 8589934592 | bytes 8388608 | tf_op jit(solution)/shard_map/pallas_call | solution.py:169
  88.3 3.7 %all-to-all-start = ((s16[128,32,128]{2,1,0:T(8,128)(2,1)}), s16[128,32,128]{2,1,0:T(8,128)(2,1)S(1)}, u32[]{:S(2)}, u32[]{:S(2)}) async-start(s16[128,32,128]{2,1,0:T(8,128)(2,1)} %get-tuple-element.12), calls=%async_computation | async-start | bytes 2097152 | tf_op jit(solution)/shard_map/all_to_all | solution.py:233
  92.0 0.1 select_reduce_fusion
  92.1 2.1 %slice_reduce_fusion = f32[128]{0:T(128)S(1)} fusion(f32[128,8,128]{2,1,0:T(8,128)} %get-tuple-element.11), kind=kLoop, calls=%fused_computation.16 | loop fusion | bytes 1024 | tf_op jit(solution)/shard_map/slice | solution.py:234
  94.2 22.4 %all-gather.1 = f32[8,1,256]{2,1,0:T(1,128)S(1)} all-gather(f32[1,1,256]{2,1,0:T(1,128)S(1)} %bitcast.47), channel_id=2, replica_groups=mesh['groups'=2,'tile'=4,'pair'=2,'sub'=2] {'tile','sub'}, dimensions={0}, use_global_device_ids=true | all-gather | bytes 9216 | tf_op jit(solution)/shard_map/all_gather | solution.py:235
  116.6 0.1 reshape.43
  116.7 0.1 reshape.44
  116.8 0.1 convert_reduce_fusion.1
  116.9 0.9 all-to-all-done
  117.8 0.5 abs_multiply_fusion
  118.3 2.3 %fusion = f32[32,4096]{1,0:T(8,128)S(1)} fusion(f32[16,8,32,128]{3,2,1,0:T(8,128)S(1)} %bitcast.38, f32[32]{0:T(128)S(1)} %broadcast_maximum_fusion, f32[128]{0:T(128)S(1)} %get-tuple-element.15, f32[128]{0:T(128)S(1)} %get-tuple-element.16), kind=kOutput, calls=%fused_computation.1 | convolution fusion | flops 201338880 | bytes 2622592 | tf_op jit(solution)/shard_map/dot_general | solution.py:245
  120.6 2.8 %collective-permute-start.1 = (f32[1,8,4096]{2,1,0:T(8,128)S(1)}, f32[1,8,4096]{2,1,0:T(8,128)S(1)}, u32[]{:S(2)}, u32[]{:S(2)}) collective-permute-start(f32[1,8,4096]{2,1,0:T(8,128)S(1)} %get-tuple-element.14), channel_id=1, source_target_pairs={{1,0},{4,1},{5,4},{8,5},{9,8},{12,9},{13,12},{3,2},{6,3},{7,6},{10... | collective-permute-start | bytes 393224 | tf_op jit(solution)/shard_map/ppermute | solution.py:31
  123.4 4.2 %collective-permute-start = (f32[1,8,4096]{2,1,0:T(8,128)S(1)}, f32[1,8,4096]{2,1,0:T(8,128)S(1)}, u32[]{:S(2)}, u32[]{:S(2)}) collective-permute-start(f32[1,8,4096]{2,1,0:T(8,128)S(1)} %get-tuple-element.13), channel_id=1, source_target_pairs={{0,1},{1,4},{4,5},{5,8},{8,9},{9,12},{12,13},{2,3},{3,6},{6,7},{7,... | collective-permute-start | bytes 393224 | tf_op jit(solution)/shard_map/ppermute | solution.py:28
  127.7 0.7 collective-permute-done.1
  128.4 1.2 collective-permute-done
  129.6 0.2 fusion.5
  129.8 0.8 reshape.47
  130.6 0.1 copy.31
  130.7 1.2 reshape.48
  (14 shorter events, 0.1 us)
Async XLA Ops:
  6.5 3.4 %copy-start = (bf16[1,64,16384]{2,1,0:T(8,128)(2,1)S(1)}, bf16[1,64,16384]{2,1,0:T(8,128)(2,1)}, u32[]{:S(2)}) copy-start(bf16[1,64,16384]{2,1,0:T(8,128)(2,1)} %param.5) | copy-start | bytes 6291460
  6.5 35.1 %all-gather.4.cloned.1.call-start = ((), (), s32[]{:S(2)}) async-start(), calls=%async_computation.1 | async-start | bytes 2359296 | tf_op jit(solution)/shard_map/all_gather | solution.py:210
  10.0 1.9 %copy-start.1 = (s32[1,64,1]{1,2,0:T(1,128)S(1)}, s32[1,64,1]{1,2,0:T(1,128)}, u32[]{:S(2)}) copy-start(s32[1,64,1]{1,2,0:T(1,128)} %param.6) | copy-start | bytes 772
  12.0 15.1 %copy-start.2 = (s32[1,64]{1,0:T(1,128)S(1)}, s32[1,64]{1,0:T(1,128)}, u32[]{:S(2)}) copy-start(s32[1,64]{1,0:T(1,128)} %param.7) | copy-start | bytes 772
  88.3 3.7 %copy-start.3 = (s32[64]{0:T(128)S(1)}, s32[64]{0:T(128)}, u32[]{:S(2)}) copy-start(s32[64]{0:T(128)} %get-tuple-element.18.places_ref) | copy-start | bytes 772
  88.3 29.5 %all-to-all-start = ((s16[128,32,128]{2,1,0:T(8,128)(2,1)}), s16[128,32,128]{2,1,0:T(8,128)(2,1)S(1)}, u32[]{:S(2)}, u32[]{:S(2)}) async-start(s16[128,32,128]{2,1,0:T(8,128)(2,1)} %get-tuple-element.12), calls=%async_computation | async-start | bytes 2097152 | tf_op jit(solution)/shard_map/all_to_all | solution.py:233
  120.6 7.8 %collective-permute-start.1 = (f32[1,8,4096]{2,1,0:T(8,128)S(1)}, f32[1,8,4096]{2,1,0:T(8,128)S(1)}, u32[]{:S(2)}, u32[]{:S(2)}) collective-permute-start(f32[1,8,4096]{2,1,0:T(8,128)S(1)} %get-tuple-element.14), channel_id=1, source_target_pairs={{1,0},{4,1},{5,4},{8,5},{9,8},{12,9},{13,12},{3,2},{6,3},{7,6},{10... | collective-permute-start | bytes 393224 | tf_op jit(solution)/shard_map/ppermute | solution.py:31
  123.4 6.2 %collective-permute-start = (f32[1,8,4096]{2,1,0:T(8,128)S(1)}, f32[1,8,4096]{2,1,0:T(8,128)S(1)}, u32[]{:S(2)}, u32[]{:S(2)}) collective-permute-start(f32[1,8,4096]{2,1,0:T(8,128)S(1)} %get-tuple-element.13), channel_id=1, source_target_pairs={{0,1},{1,4},{4,5},{5,8},{8,9},{9,12},{12,13},{2,3},{3,6},{6,7},{7,... | collective-permute-start | bytes 393224 | tf_op jit(solution)/shard_map/ppermute | solution.py:28
Sparse Core Ops, SparseCore 0:
  10.1 31.5 all-gather.3

commit v4 on v2

--- a/solution.py
+++ b/solution.py
@@ -15,6 +15,7 @@
 PHASES = 4
 DEPTH = 80
 EACH = 2
+SUMMED = 4
 
 epsilon = 1e-06
 
@@ -59,12 +60,12 @@
 def patches(windows):
     amount = windows.shape[0]
     surface = jax.ShapeDtypeStruct((amount, CHIP, LANES), jnp.float32)
-    block = pl.BlockSpec((EACH, CHIP, LANES), lambda i: (i, 0, 0))
+    block = pl.BlockSpec((SUMMED, CHIP, LANES), lambda i: (i, 0, 0))
     return pl.pallas_call(
         patch_kernel,
         out_shape=(surface, surface),
-        grid=(amount // EACH,),
-        in_specs=[pl.BlockSpec((EACH, WIN, WIN), lambda i: (i, 0, 0))],
+        grid=(amount // SUMMED,),
+        in_specs=[pl.BlockSpec((SUMMED, WIN, WIN), lambda i: (i, 0, 0))],
         out_specs=(block, block),
         cost_estimate=pl.CostEstimate(
             flops=amount * 2 * 128 * 512 * 256, bytes_accessed=40 * 1024 * 1024, transcendentals=0
@@ -184,7 +185,7 @@
                 pltpu.VMEM((EACH, PHASES, WIN, LANES), jnp.bfloat16),
             ],
         ),
-        compiler_params=pltpu.CompilerParams(vmem_limit_bytes=40 * 1024 * 1024),
+        compiler_params=pltpu.CompilerParams(vmem_limit_bytes=58 * 1024 * 1024),
         cost_estimate=pl.CostEstimate(
             flops=amount * 2 * 128 * 512 * 1024, bytes_accessed=8 * 1024 * 1024, transcendentals=0
         ),

time: 135 us -> 131 us (0.970)
  the two profiles are of different devices: /device:TPU:30 before, /device:TPU:1 now
where the time goes in v4:
time: 131 us; the launch traced here: 129 us
  Pallas kernels  51.8 us (40%)
  blocking collectives  22.4 us (17%)
  waiting for transfers between devices  16.8 us (13%)
  between operations  13.5 us (10%)
  starting transfers between devices  10.9 us (8%)
  local copies, waits for them, and re-layouts  9.58 us (7%)
  matrix products  2.32 us (2%)
  other arithmetic  1.67 us (1%)
    pallas_call x1, Pallas kernels, match(): pl.pallas_call(match_kernel, out_shape=(jax.ShapeDtypeStruct((slot_amount...  36.7 us
    all_gather x1, blocking collectives, on_device(): lax.all_gather(notes, axes, axis=0).reshape(devices, 2, devices, capacity)  22.4 us
    pallas_call x1, Pallas kernels, patches(): pl.pallas_call(patch_kernel, out_shape=(surface, surface), grid=(amount /...  15.1 us
    all_gather x1, waiting for transfers between devices, on_device(): lax.all_gather(turned.reshape(chip_amount, half, LANES), axes, axis=0, ti...  14 us
    ppermute x1, starting transfers between devices, padded(): lax.ppermute(lax.slice_in_dim(block, block.shape[dim] - width, None, axis...  4.25 us
    all_to_all x1, starting transfers between devices, on_device(): codes = lax.all_to_all(codes, axes, split_axis=0, concat_axis=0, tiled=True)  3.86 us
    ppermute x1, starting transfers between devices, padded(): lax.ppermute(lax.slice_in_dim(block, 0, width, axis=dim), axis, backward)  2.79 us
  transfers between devices with their start and end apart: 4, of which 4 were waited for; matrix products, arithmetic and copies ran while one was open for 4% of the time, Pallas kernels for 12%

profile of v4, /device:TPU:1, one launch (start us, length us, event | category | flops | bytes accessed | tf_op | source)
XLA Modules:
  0.0 128.9 jit_solution(17267854186220988898)
XLA Ops:
  6.5 1.6 %reshape_squeeze.6 = bf16[32,64,64]{2,1,0:T(8,128)(2,1)S(1)} reshape(bf16[1,32,4096]{2,1,0:T(8,128)(2,1)} %param.4) | data formatting | bytes 524288 | tf_op jit(solution)/shard_map/reshape;squeeze | solution.py:208
  8.2 0.3 copy.19
  8.4 0.5 copy.20
  9.0 1.0 reshape.42
  9.9 0.0 all-gather.4.cloned.1.call-update
  10.0 0.0 copy-start.1
  10.0 1.9 %copy.23 = bf16[8,8,128,128]{3,2,1,0:T(8,128)(2,1)} copy(bf16[8,8,128,128]{3,1,2,0:T(8,128)(2,1)S(1)} %bitcast.41) | data formatting | bytes 4194304
  11.9 0.2 convert_reduce_fusion
  12.0 0.0 copy-start.2
  12.0 15.1 %shard_map.46 = (f32[64,64,128]{2,1,0:T(8,128)}, f32[64,64,128]{2,1,0:T(8,128)}) custom-call(bf16[64,128,128]{2,1,0:T(8,128)(2,1)} %bitcast.42), custom_call_target="tpu_custom_call" | custom-call | flops 2147483648 | bytes 41943040 | tf_op jit(solution)/shard_map/pallas_call | solution.py:64
  27.1 0.6 multiply_add_fusion
  27.7 14.0 %all-gather.4.cloned.1.call-done.refs_0_.refs_1_ = bf16[256,32,128]{2,1,0:T(8,128)(2,1)} async-done(((bf16[32,32,128]{2,1,0:T(8,128)(2,1)}), bf16[256,32,128]{2,1,0:T(8,128)(2,1)}) %all-gather.4.cloned.1.call-update) | async-done | bytes 2097168 | tf_op jit(solution)/shard_map/all_gather | solution.py:210
  41.7 36.7 %shard_map.47 = (s16[128,32,128]{2,1,0:T(8,128)(2,1)}, f32[128,8,128]{2,1,0:T(8,128)}) custom-call(s32[64]{0:T(128)} %get-tuple-element.18.places_ref, s32[64]{0:T(128)} %get-tuple-element.17.names_ref, bf16[256,32,128]{2,1,0:T(8,128)(2,1)} %all-gather.4.cloned.1.call-done.refs_0_.refs_1_, ...), custom_call_target="tpu_custom_call" | custom-call | flops 8589934592 | bytes 8388608 | tf_op jit(solution)/shard_map/pallas_call | solution.py:168
  78.4 3.9 %all-to-all-start = ((s16[128,32,128]{2,1,0:T(8,128)(2,1)}), s16[128,32,128]{2,1,0:T(8,128)(2,1)S(1)}, u32[]{:S(2)}, u32[]{:S(2)}) async-start(s16[128,32,128]{2,1,0:T(8,128)(2,1)} %get-tuple-element.12), calls=%async_computation | async-start | bytes 2097152 | tf_op jit(solution)/shard_map/all_to_all | solution.py:233
  82.2 0.0 copy-done.3
  82.2 0.1 select_reduce_fusion
  82.4 2.1 %slice_reduce_fusion = f32[128]{0:T(128)S(1)} fusion(f32[128,8,128]{2,1,0:T(8,128)} %get-tuple-element.11), kind=kLoop, calls=%fused_computation.16 | loop fusion | bytes 1024 | tf_op jit(solution)/shard_map/slice | solution.py:234
  84.4 22.4 %all-gather.1 = f32[8,1,256]{2,1,0:T(1,128)S(1)} all-gather(f32[1,1,256]{2,1,0:T(1,128)S(1)} %bitcast.47), channel_id=2, replica_groups=mesh['groups'=2,'tile'=4,'pair'=2,'sub'=2] {'tile','sub'}, dimensions={0}, use_global_device_ids=true | all-gather | bytes 9216 | tf_op jit(solution)/shard_map/all_gather | solution.py:235
  106.9 0.1 reshape.43
  107.0 0.1 reshape.44
  107.1 0.1 convert_reduce_fusion.1
  107.2 0.9 all-to-all-done
  108.0 0.5 abs_multiply_fusion
  108.5 2.3 %fusion = f32[32,4096]{1,0:T(8,128)S(1)} fusion(f32[16,8,32,128]{3,2,1,0:T(8,128)S(1)} %bitcast.38, f32[32]{0:T(128)S(1)} %broadcast_maximum_fusion, f32[128]{0:T(128)S(1)} %get-tuple-element.15, f32[128]{0:T(128)S(1)} %get-tuple-element.16), kind=kOutput, calls=%fused_computation.1 | convolution fusion | flops 201338880 | bytes 2622592 | tf_op jit(solution)/shard_map/dot_general | solution.py:245
  110.9 2.8 %collective-permute-start.1 = (f32[1,8,4096]{2,1,0:T(8,128)S(1)}, f32[1,8,4096]{2,1,0:T(8,128)S(1)}, u32[]{:S(2)}, u32[]{:S(2)}) collective-permute-start(f32[1,8,4096]{2,1,0:T(8,128)S(1)} %get-tuple-element.14), channel_id=1, source_target_pairs={{1,0},{4,1},{5,4},{8,5},{9,8},{12,9},{13,12},{3,2},{6,3},{7,6},{10... | collective-permute-start | bytes 393224 | tf_op jit(solution)/shard_map/ppermute | solution.py:31
  113.7 4.2 %collective-permute-start = (f32[1,8,4096]{2,1,0:T(8,128)S(1)}, f32[1,8,4096]{2,1,0:T(8,128)S(1)}, u32[]{:S(2)}, u32[]{:S(2)}) collective-permute-start(f32[1,8,4096]{2,1,0:T(8,128)S(1)} %get-tuple-element.13), channel_id=1, source_target_pairs={{0,1},{1,4},{4,5},{5,8},{8,9},{9,12},{12,13},{2,3},{3,6},{6,7},{7,... | collective-permute-start | bytes 393224 | tf_op jit(solution)/shard_map/ppermute | solution.py:28
  117.9 0.7 collective-permute-done.1
  118.6 1.2 collective-permute-done
  119.9 0.2 fusion.5
  120.0 0.8 reshape.47
  120.8 0.1 copy.31
  120.9 1.2 reshape.48
  (14 shorter events, 0.1 us)
Async XLA Ops:
  6.5 3.4 %copy-start = (bf16[1,64,16384]{2,1,0:T(8,128)(2,1)S(1)}, bf16[1,64,16384]{2,1,0:T(8,128)(2,1)}, u32[]{:S(2)}) copy-start(bf16[1,64,16384]{2,1,0:T(8,128)(2,1)} %param.5) | copy-start | bytes 6291460
  6.5 35.1 %all-gather.4.cloned.1.call-start = ((), (), s32[]{:S(2)}) async-start(), calls=%async_computation.1 | async-start | bytes 2359296 | tf_op jit(solution)/shard_map/all_gather | solution.py:210
  10.0 1.9 %copy-start.1 = (s32[1,64,1]{1,2,0:T(1,128)S(1)}, s32[1,64,1]{1,2,0:T(1,128)}, u32[]{:S(2)}) copy-start(s32[1,64,1]{1,2,0:T(1,128)} %param.6) | copy-start | bytes 772
  12.0 15.1 %copy-start.2 = (s32[1,64]{1,0:T(1,128)S(1)}, s32[1,64]{1,0:T(1,128)}, u32[]{:S(2)}) copy-start(s32[1,64]{1,0:T(1,128)} %param.7) | copy-start | bytes 772
  78.4 3.9 %copy-start.3 = (s32[64]{0:T(128)S(1)}, s32[64]{0:T(128)}, u32[]{:S(2)}) copy-start(s32[64]{0:T(128)} %get-tuple-element.18.places_ref) | copy-start | bytes 772
  78.4 29.7 %all-to-all-start = ((s16[128,32,128]{2,1,0:T(8,128)(2,1)}), s16[128,32,128]{2,1,0:T(8,128)(2,1)S(1)}, u32[]{:S(2)}, u32[]{:S(2)}) async-start(s16[128,32,128]{2,1,0:T(8,128)(2,1)} %get-tuple-element.12), calls=%async_computation | async-start | bytes 2097152 | tf_op jit(solution)/shard_map/all_to_all | solution.py:233
  110.9 7.8 %collective-permute-start.1 = (f32[1,8,4096]{2,1,0:T(8,128)S(1)}, f32[1,8,4096]{2,1,0:T(8,128)S(1)}, u32[]{:S(2)}, u32[]{:S(2)}) collective-permute-start(f32[1,8,4096]{2,1,0:T(8,128)S(1)} %get-tuple-element.14), channel_id=1, source_target_pairs={{1,0},{4,1},{5,4},{8,5},{9,8},{12,9},{13,12},{3,2},{6,3},{7,6},{10... | collective-permute-start | bytes 393224 | tf_op jit(solution)/shard_map/ppermute | solution.py:31
  113.7 6.2 %collective-permute-start = (f32[1,8,4096]{2,1,0:T(8,128)S(1)}, f32[1,8,4096]{2,1,0:T(8,128)S(1)}, u32[]{:S(2)}, u32[]{:S(2)}) collective-permute-start(f32[1,8,4096]{2,1,0:T(8,128)S(1)} %get-tuple-element.13), channel_id=1, source_target_pairs={{0,1},{1,4},{4,5},{5,8},{8,9},{9,12},{12,13},{2,3},{3,6},{6,7},{7,... | collective-permute-start | bytes 393224 | tf_op jit(solution)/shard_map/ppermute | solution.py:28
Sparse Core Ops, SparseCore 0:
  10.1 31.5 all-gather.3

commit v5 on v4

--- a/solution.py
+++ b/solution.py
@@ -46,13 +46,17 @@
     return image
 
 
-def patch_kernel(windows_ref, first_ref, inverse_ref):
+def patch_kernel(windows_ref, first_ref, inverse_ref, copies_ref):
     for item in range(windows_ref.shape[0]):
         window = windows_ref[item].astype(jnp.float32)
         first = box_sums(window)
         second = box_sums(window * window)
         patch_mean = first / (CHIP * CHIP)
         patch_var = second / (CHIP * CHIP) - patch_mean * patch_mean
+        for phase in range(PHASES):
+            moved = window if phase == 0 else pltpu.roll(window, WIN - phase, 1)
+            copies_ref[item, 0, phase] = moved.astype(jnp.bfloat16)
+            copies_ref[item, 1, phase] = pltpu.roll(moved, WIN - SUBLANES, 0).astype(jnp.bfloat16)
         first_ref[item] = first
         inverse_ref[item] = 1.0 / (CHIP * jnp.sqrt(patch_var + epsilon))
 
@@ -63,17 +67,26 @@
     block = pl.BlockSpec((SUMMED, CHIP, LANES), lambda i: (i, 0, 0))
     return pl.pallas_call(
         patch_kernel,
-        out_shape=(surface, surface),
+        out_shape=(
+            surface,
+            surface,
+            jax.ShapeDtypeStruct((amount, 2, PHASES, WIN, LANES), jnp.bfloat16),
+        ),
         grid=(amount // SUMMED,),
         in_specs=[pl.BlockSpec((SUMMED, WIN, WIN), lambda i: (i, 0, 0))],
-        out_specs=(block, block),
+        out_specs=(
+            block,
+            block,
+            pl.BlockSpec((SUMMED, 2, PHASES, WIN, LANES), lambda i: (i, 0, 0, 0, 0)),
+        ),
+        compiler_params=pltpu.CompilerParams(vmem_limit_bytes=40 * 1024 * 1024),
         cost_estimate=pl.CostEstimate(
             flops=amount * 2 * 128 * 512 * 256, bytes_accessed=40 * 1024 * 1024, transcendentals=0
         ),
     )(windows)
 
 
-def correlate(chip_ref, window_ref, first_ref, inverse_ref, even_ref, odd_ref):
+def correlate(chip_ref, first_ref, inverse_ref, even_ref, odd_ref):
     half = CHIP // 2
     chip = chip_ref[...].astype(jnp.float32)
     total = jnp.sum(jnp.sum(chip, axis=0, keepdims=True), axis=1, keepdims=True)
@@ -93,12 +106,6 @@
             rows.append(pltpu.roll(row, 0, 1, stride=1, stride_axis=0))
         left.append(jnp.concatenate(rows, axis=0).astype(jnp.bfloat16)[:, :DEPTH])
     left = jnp.concatenate(left, axis=1)
-
-    window = window_ref[...].astype(jnp.float32)
-    for phase in range(PHASES):
-        moved = window if phase == 0 else pltpu.roll(window, WIN - phase, 1)
-        even_ref[phase] = moved.astype(jnp.bfloat16)
-        odd_ref[phase] = pltpu.roll(moved, WIN - SUBLANES, 0).astype(jnp.bfloat16)
 
     groups = CHIP // SUBLANES
     surfaces = []
@@ -125,7 +132,7 @@
 
 def match_kernel(places_ref, names_ref, *refs):
     chips, rest = refs[:EACH], refs[EACH:]
-    windows_ref, first_ref, inverse_ref, out_ref, scale_ref, even_ref, odd_ref = rest
+    copies_ref, first_ref, inverse_ref, out_ref, scale_ref = rest
     step = pl.program_id(0)
 
     @pl.when(step == 0)
@@ -138,11 +145,10 @@
     for item in range(EACH):
         score = correlate(
             chips[item].at[0],
-            windows_ref.at[item],
             first_ref.at[item],
             inverse_ref.at[item],
-            even_ref.at[item],
-            odd_ref.at[item],
+            copies_ref.at[item, 0],
+            copies_ref.at[item, 1],
         )
         low, high = score[:half], pltpu.roll(score[half:], CHIP, 1)
         packed = jnp.where(lane < CHIP, low, high)
@@ -157,8 +163,8 @@
         scale_ref[place] = jnp.broadcast_to(largest, (SUBLANES, LANES))
 
 
-def match(positions, names, everyone, windows, first, inverse, slot_amount):
-    amount = windows.shape[0]
+def match(positions, names, everyone, copies, first, inverse, slot_amount):
+    amount = copies.shape[0]
     half = CHIP // 2
 
     def chip_spec(item):
@@ -175,21 +181,21 @@
             num_scalar_prefetch=2,
             grid=(amount // EACH,),
             in_specs=[chip_spec(item) for item in range(EACH)]
-            + [pl.BlockSpec((EACH, WIN, WIN), lambda i, p, n: (i, 0, 0)), surface, surface],
+            + [
+                pl.BlockSpec((EACH, 2, PHASES, WIN, LANES), lambda i, p, n: (i, 0, 0, 0, 0)),
+                surface,
+                surface,
+            ],
             out_specs=(
                 pl.BlockSpec((slot_amount, half, LANES), lambda i, p, n: (0, 0, 0)),
                 pl.BlockSpec((slot_amount, SUBLANES, LANES), lambda i, p, n: (0, 0, 0)),
             ),
-            scratch_shapes=[
-                pltpu.VMEM((EACH, PHASES, WIN, LANES), jnp.bfloat16),
-                pltpu.VMEM((EACH, PHASES, WIN, LANES), jnp.bfloat16),
-            ],
         ),
         compiler_params=pltpu.CompilerParams(vmem_limit_bytes=58 * 1024 * 1024),
         cost_estimate=pl.CostEstimate(
             flops=amount * 2 * 128 * 512 * 1024, bytes_accessed=8 * 1024 * 1024, transcendentals=0
         ),
-    )(positions, names, *([everyone] * EACH), windows, first, inverse)
+    )(positions, names, *([everyone] * EACH), copies, first, inverse)
 
 
 def on_device(ref_chips, search_windows, dest_block, dest_slot):
@@ -220,12 +226,12 @@
     )
 
     windows = windows.reshape(window_amount, WIN, WIN)
-    first, inverse = patches(windows)
+    first, inverse, copies = patches(windows)
     codes, scales = match(
         positions,
         targets * chip_amount + target_slot,
         everyone,
-        windows,
+        copies,
         first,
         inverse,
         slot_amount,

time: 131 us -> 132 us (level)
  Pallas kernels: 51.8 us -> 56.9 us
  waiting for transfers between devices: 16.8 us -> 12.4 us
  local copies, waits for them, and re-layouts: 9.58 us -> 10.9 us
    all_gather x1, waiting for transfers between devices: 14 us -> 7.13 us  [on_device(): lax.all_gather(turned.reshape(chip_amount, half, LANES), axes, axis=0, ti...]
    pallas_call x1, Pallas kernels: 15.1 us -> 20.5 us  [patches(): pl.pallas_call(patch_kernel, out_shape=(surface, surface, jax.ShapeDtypeS...]
    ppermute x1, waiting for transfers between devices: 0.71 us -> 4.35 us  [padded(): lax.ppermute(lax.slice_in_dim(block, 0, width, axis=dim), axis, backward)]
    unnamed x9 -> x13, local copies, waits for them, and re-layouts: 1.9 us -> 3.27 us
  transfers between devices with their start and end apart: 4 -> 4, of which waited for: 4 -> 3; matrix products, arithmetic and copies ran while one was open for 4% -> 3% of each run, Pallas kernels for 12% -> 16%
where the time goes in v5:
time: 132 us; the launch traced here: 131 us
  Pallas kernels  56.9 us (43%)
  blocking collectives  22.4 us (17%)
  between operations  13.6 us (10%)
  waiting for transfers between devices  12.4 us (9%)
  local copies, waits for them, and re-layouts  10.9 us (8%)
  starting transfers between devices  10.9 us (8%)
  matrix products  2.32 us (2%)
  other arithmetic  1.67 us (1%)
    pallas_call x1, Pallas kernels, match(): pl.pallas_call(match_kernel, out_shape=(jax.ShapeDtypeStruct((slot_amount...  36.4 us
    all_gather x1, blocking collectives, on_device(): lax.all_gather(notes, axes, axis=0).reshape(devices, 2, devices, capacity)  22.4 us
    pallas_call x1, Pallas kernels, patches(): pl.pallas_call(patch_kernel, out_shape=(surface, surface, jax.ShapeDtypeS...  20.5 us
    all_gather x1, waiting for transfers between devices, on_device(): lax.all_gather(turned.reshape(chip_amount, half, LANES), axes, axis=0, ti...  7.13 us
    ppermute x1, starting transfers between devices, padded(): lax.ppermute(lax.slice_in_dim(block, block.shape[dim] - width, None, axis...  5.12 us
    ppermute x1, waiting for transfers between devices, padded(): lax.ppermute(lax.slice_in_dim(block, 0, width, axis=dim), axis, backward)  4.35 us
    all_to_all x1, starting transfers between devices, on_device(): codes = lax.all_to_all(codes, axes, split_axis=0, concat_axis=0, tiled=True)  3.87 us
    unnamed x13, local copies, waits for them, and re-layouts  3.27 us
  transfers between devices with their start and end apart: 4, of which 3 were waited for; matrix products, arithmetic and copies ran while one was open for 3% of the time, Pallas kernels for 16%

profile of v5, /device:TPU:1, one launch (start us, length us, event | category | flops | bytes accessed | tf_op | source)
XLA Modules:
  0.0 131.0 jit_solution(10268111953078920874)
XLA Ops:
  6.5 1.6 %reshape_squeeze.6 = bf16[32,64,64]{2,1,0:T(8,128)(2,1)S(1)} reshape(bf16[1,32,4096]{2,1,0:T(8,128)(2,1)} %param.4) | data formatting | bytes 524288 | tf_op jit(solution)/shard_map/reshape;squeeze | solution.py:214
  8.2 0.3 copy.19
  8.4 0.5 copy.20
  9.0 1.0 reshape.42
  9.9 0.0 all-gather.4.cloned.1.call-update
  10.0 0.0 copy-start.3
  10.0 0.6 copy.23
  10.5 0.1 copy-done.3
  10.6 0.2 convert_reduce_fusion
  10.8 20.5 %shard_map.46 = (f32[64,64,128]{2,1,0:T(8,128)S(1)}, f32[64,64,128]{2,1,0:T(8,128)S(1)}, bf16[64,2,4,128,128]{4,3,2,1,0:T(8,128)(2,1)}) custom-call(bf16[64,128,128]{2,1,0:T(8,128)(2,1)S(1)} %bitcast.38), custom_call_target="tpu_custom_call" | custom-call | flops 2147483648 | bytes 41943040 | tf_op jit(solution)/shard_map/pallas_call | solution.py:68
  31.3 1.3 copy-done
  32.6 1.3 copy-done.1
  33.9 0.6 multiply_add_fusion
  34.5 7.1 %all-gather.4.cloned.1.call-done.refs_0_.refs_1_ = bf16[256,32,128]{2,1,0:T(8,128)(2,1)} async-done(((bf16[32,32,128]{2,1,0:T(8,128)(2,1)}), bf16[256,32,128]{2,1,0:T(8,128)(2,1)}) %all-gather.4.cloned.1.call-update) | async-done | bytes 2097168 | tf_op jit(solution)/shard_map/all_gather | solution.py:216
  41.7 36.4 %shard_map.47 = (s16[128,32,128]{2,1,0:T(8,128)(2,1)}, f32[128,8,128]{2,1,0:T(8,128)}) custom-call(s32[64]{0:T(128)} %get-tuple-element.20.places_ref, s32[64]{0:T(128)} %get-tuple-element.19.names_ref, bf16[256,32,128]{2,1,0:T(8,128)(2,1)} %all-gather.4.cloned.1.call-done.refs_0_.refs_1_, ...), custom_call_target="tpu_custom_call" | custom-call | flops 8589934592 | bytes 8388608 | tf_op jit(solution)/shard_map/pallas_call | solution.py:174
  78.0 3.9 %all-to-all-start = ((s16[128,32,128]{2,1,0:T(8,128)(2,1)}), s16[128,32,128]{2,1,0:T(8,128)(2,1)S(1)}, u32[]{:S(2)}, u32[]{:S(2)}) async-start(s16[128,32,128]{2,1,0:T(8,128)(2,1)} %get-tuple-element.14), calls=%async_computation | async-start | bytes 2097152 | tf_op jit(solution)/shard_map/all_to_all | solution.py:239
  81.9 0.1 select_reduce_fusion
  82.0 2.1 %slice_reduce_fusion = f32[128]{0:T(128)S(1)} fusion(f32[128,8,128]{2,1,0:T(8,128)} %get-tuple-element.13), kind=kLoop, calls=%fused_computation.16 | loop fusion | bytes 1024 | tf_op jit(solution)/shard_map/slice | solution.py:240
  84.1 22.4 %all-gather.1 = f32[8,1,256]{2,1,0:T(1,128)S(1)} all-gather(f32[1,1,256]{2,1,0:T(1,128)S(1)} %bitcast.46), channel_id=2, replica_groups=mesh['groups'=2,'tile'=4,'pair'=2,'sub'=2] {'tile','sub'}, dimensions={0}, use_global_device_ids=true | all-gather | bytes 9216 | tf_op jit(solution)/shard_map/all_gather | solution.py:241
  106.5 0.1 reshape.43
  106.6 0.1 reshape.44
  106.7 0.1 convert_reduce_fusion.1
  106.9 0.9 all-to-all-done
  107.7 0.5 abs_multiply_fusion
  108.2 2.3 %fusion = f32[32,4096]{1,0:T(8,128)S(1)} fusion(f32[16,8,32,128]{3,2,1,0:T(8,128)S(1)} %bitcast.39, f32[32]{0:T(128)S(1)} %broadcast_maximum_fusion, f32[128]{0:T(128)S(1)} %get-tuple-element.17, f32[128]{0:T(128)S(1)} %get-tuple-element.18), kind=kOutput, calls=%fused_computation.1 | convolution fusion | flops 201338880 | bytes 2622592 | tf_op jit(solution)/shard_map/dot_general | solution.py:251
  110.5 5.1 %collective-permute-start = (f32[1,8,4096]{2,1,0:T(8,128)S(1)}, f32[1,8,4096]{2,1,0:T(8,128)S(1)}, u32[]{:S(2)}, u32[]{:S(2)}) collective-permute-start(f32[1,8,4096]{2,1,0:T(8,128)S(1)} %get-tuple-element.15), channel_id=1, source_target_pairs={{0,1},{1,4},{4,5},{5,8},{8,9},{9,12},{12,13},{2,3},{3,6},{6,7},{7,... | collective-permute-start | bytes 393224 | tf_op jit(solution)/shard_map/ppermute | solution.py:28
  115.7 1.9 %collective-permute-start.1 = (f32[1,8,4096]{2,1,0:T(8,128)S(1)}, f32[1,8,4096]{2,1,0:T(8,128)S(1)}, u32[]{:S(2)}, u32[]{:S(2)}) collective-permute-start(f32[1,8,4096]{2,1,0:T(8,128)S(1)} %get-tuple-element.16), channel_id=1, source_target_pairs={{1,0},{4,1},{5,4},{8,5},{9,8},{12,9},{13,12},{3,2},{6,3},{7,6},{10... | collective-permute-start | bytes 393224 | tf_op jit(solution)/shard_map/ppermute | solution.py:31
  117.6 4.3 %collective-permute-done.1 = f32[1,8,4096]{2,1,0:T(8,128)S(1)} collective-permute-done((f32[1,8,4096]{2,1,0:T(8,128)S(1)}, f32[1,8,4096]{2,1,0:T(8,128)S(1)}, u32[]{:S(2)}, u32[]{:S(2)}) %collective-permute-start.1) | collective-permute-done | bytes 131104 | tf_op jit(solution)/shard_map/ppermute | solution.py:31
  122.0 0.2 fusion.5
  122.1 0.8 reshape.47
  122.9 0.1 copy.31
  123.0 1.2 reshape.48
  (18 shorter events, 0.1 us)
Async XLA Ops:
  6.5 3.4 %copy-start.2 = (bf16[1,64,16384]{2,1,0:T(8,128)(2,1)S(1)}, bf16[1,64,16384]{2,1,0:T(8,128)(2,1)}, u32[]{:S(2)}) copy-start(bf16[1,64,16384]{2,1,0:T(8,128)(2,1)} %param.5) | copy-start | bytes 6291460
  6.5 35.1 %all-gather.4.cloned.1.call-start = ((), (), s32[]{:S(2)}) async-start(), calls=%async_computation.1 | async-start | bytes 2359296 | tf_op jit(solution)/shard_map/all_gather | solution.py:216
  10.0 0.7 copy-start.3
  10.8 23.1 %copy-start.4 = (s32[1,64]{1,0:T(1,128)S(1)}, s32[1,64]{1,0:T(1,128)}, u32[]{:S(2)}) copy-start(s32[1,64]{1,0:T(1,128)} %param.7) | copy-start | bytes 772
  31.3 1.3 copy-start
  32.6 1.3 copy-start.1
  78.0 3.9 %copy-start.5 = (s32[64]{0:T(128)S(1)}, s32[64]{0:T(128)}, u32[]{:S(2)}) copy-start(s32[64]{0:T(128)} %get-tuple-element.20.places_ref) | copy-start | bytes 772
  78.0 29.7 %all-to-all-start = ((s16[128,32,128]{2,1,0:T(8,128)(2,1)}), s16[128,32,128]{2,1,0:T(8,128)(2,1)S(1)}, u32[]{:S(2)}, u32[]{:S(2)}) async-start(s16[128,32,128]{2,1,0:T(8,128)(2,1)} %get-tuple-element.14), calls=%async_computation | async-start | bytes 2097152 | tf_op jit(solution)/shard_map/all_to_all | solution.py:239
  110.5 7.1 %collective-permute-start = (f32[1,8,4096]{2,1,0:T(8,128)S(1)}, f32[1,8,4096]{2,1,0:T(8,128)S(1)}, u32[]{:S(2)}, u32[]{:S(2)}) collective-permute-start(f32[1,8,4096]{2,1,0:T(8,128)S(1)} %get-tuple-element.15), channel_id=1, source_target_pairs={{0,1},{1,4},{4,5},{5,8},{8,9},{9,12},{12,13},{2,3},{3,6},{6,7},{7,... | collective-permute-start | bytes 393224 | tf_op jit(solution)/shard_map/ppermute | solution.py:28
  115.7 6.3 %collective-permute-start.1 = (f32[1,8,4096]{2,1,0:T(8,128)S(1)}, f32[1,8,4096]{2,1,0:T(8,128)S(1)}, u32[]{:S(2)}, u32[]{:S(2)}) collective-permute-start(f32[1,8,4096]{2,1,0:T(8,128)S(1)} %get-tuple-element.16), channel_id=1, source_target_pairs={{1,0},{4,1},{5,4},{8,5},{9,8},{12,9},{13,12},{3,2},{6,3},{7,6},{10... | collective-permute-start | bytes 393224 | tf_op jit(solution)/shard_map/ppermute | solution.py:31
Sparse Core Ops, SparseCore 0:
  10.1 31.5 all-gather.3

commit v6 on v4

--- a/solution.py
+++ b/solution.py
@@ -12,7 +12,7 @@
 GC = 8
 LANES = 128
 SUBLANES = 8
-PHASES = 4
+PHASES = 8
 DEPTH = 80
 EACH = 2
 SUMMED = 4

time: 131 us -> 134 us (1.023)
  Pallas kernels: 51.8 us -> 54.9 us
    pallas_call x1, Pallas kernels: 36.7 us -> 39.9 us  [match(): pl.pallas_call(match_kernel, out_shape=(jax.ShapeDtypeStruct((slot_amount...]
  transfers between devices with their start and end apart: 4 -> 4, of which waited for: 4 -> 4; matrix products, arithmetic and copies ran while one was open for 4% -> 4% of each run, Pallas kernels for 12% -> 11%
where the time goes in v6:
time: 134 us; the launch traced here: 132 us
  Pallas kernels  54.9 us (41%)
  blocking collectives  22.4 us (17%)
  waiting for transfers between devices  16.8 us (13%)
  between operations  13.5 us (10%)
  starting transfers between devices  10.9 us (8%)
  local copies, waits for them, and re-layouts  9.58 us (7%)
  matrix products  2.32 us (2%)
  other arithmetic  1.67 us (1%)
    pallas_call x1, Pallas kernels, match(): pl.pallas_call(match_kernel, out_shape=(jax.ShapeDtypeStruct((slot_amount...  39.9 us
    all_gather x1, blocking collectives, on_device(): lax.all_gather(notes, axes, axis=0).reshape(devices, 2, devices, capacity)  22.4 us
    pallas_call x1, Pallas kernels, patches(): pl.pallas_call(patch_kernel, out_shape=(surface, surface), grid=(amount /...  15.1 us
    all_gather x1, waiting for transfers between devices, on_device(): lax.all_gather(turned.reshape(chip_amount, half, LANES), axes, axis=0, ti...  14 us
    ppermute x1, starting transfers between devices, padded(): lax.ppermute(lax.slice_in_dim(block, block.shape[dim] - width, None, axis...  4.24 us
    all_to_all x1, starting transfers between devices, on_device(): codes = lax.all_to_all(codes, axes, split_axis=0, concat_axis=0, tiled=True)  3.87 us
    ppermute x1, starting transfers between devices, padded(): lax.ppermute(lax.slice_in_dim(block, 0, width, axis=dim), axis, backward)  2.79 us
  transfers between devices with their start and end apart: 4, of which 4 were waited for; matrix products, arithmetic and copies ran while one was open for 4% of the time, Pallas kernels for 11%

profile of v6, /device:TPU:1, one launch (start us, length us, event | category | flops | bytes accessed | tf_op | source)
XLA Modules:
  0.0 132.1 jit_solution(18253905292092672975)
XLA Ops:
  6.5 0.0 all-gather.4.cloned.1.call-start
  6.5 1.6 %reshape_squeeze.6 = bf16[32,64,64]{2,1,0:T(8,128)(2,1)S(1)} reshape(bf16[1,32,4096]{2,1,0:T(8,128)(2,1)} %param.4) | data formatting | bytes 524288 | tf_op jit(solution)/shard_map/reshape;squeeze | solution.py:208
  8.2 0.3 copy.19
  8.4 0.5 copy.20
  9.0 1.0 reshape.42
  9.9 0.0 all-gather.4.cloned.1.call-update
  10.0 0.0 copy-start.1
  10.0 1.9 %copy.23 = bf16[8,8,128,128]{3,2,1,0:T(8,128)(2,1)} copy(bf16[8,8,128,128]{3,1,2,0:T(8,128)(2,1)S(1)} %bitcast.41) | data formatting | bytes 4194304
  11.9 0.2 convert_reduce_fusion
  12.0 0.0 copy-start.2
  12.0 15.1 %shard_map.46 = (f32[64,64,128]{2,1,0:T(8,128)}, f32[64,64,128]{2,1,0:T(8,128)}) custom-call(bf16[64,128,128]{2,1,0:T(8,128)(2,1)} %bitcast.42), custom_call_target="tpu_custom_call" | custom-call | flops 2147483648 | bytes 41943040 | tf_op jit(solution)/shard_map/pallas_call | solution.py:64
  27.1 0.6 multiply_add_fusion
  27.7 14.0 %all-gather.4.cloned.1.call-done.refs_0_.refs_1_ = bf16[256,32,128]{2,1,0:T(8,128)(2,1)} async-done(((bf16[32,32,128]{2,1,0:T(8,128)(2,1)}), bf16[256,32,128]{2,1,0:T(8,128)(2,1)}) %all-gather.4.cloned.1.call-update) | async-done | bytes 2097168 | tf_op jit(solution)/shard_map/all_gather | solution.py:210
  41.7 39.9 %shard_map.47 = (s16[128,32,128]{2,1,0:T(8,128)(2,1)}, f32[128,8,128]{2,1,0:T(8,128)}) custom-call(s32[64]{0:T(128)} %get-tuple-element.18.places_ref, s32[64]{0:T(128)} %get-tuple-element.17.names_ref, bf16[256,32,128]{2,1,0:T(8,128)(2,1)} %all-gather.4.cloned.1.call-done.refs_0_.refs_1_, ...), custom_call_target="tpu_custom_call" | custom-call | flops 8589934592 | bytes 8388608 | tf_op jit(solution)/shard_map/pallas_call | solution.py:168
  81.5 3.9 %all-to-all-start = ((s16[128,32,128]{2,1,0:T(8,128)(2,1)}), s16[128,32,128]{2,1,0:T(8,128)(2,1)S(1)}, u32[]{:S(2)}, u32[]{:S(2)}) async-start(s16[128,32,128]{2,1,0:T(8,128)(2,1)} %get-tuple-element.12), calls=%async_computation | async-start | bytes 2097152 | tf_op jit(solution)/shard_map/all_to_all | solution.py:233
  85.4 0.1 select_reduce_fusion
  85.5 2.1 %slice_reduce_fusion = f32[128]{0:T(128)S(1)} fusion(f32[128,8,128]{2,1,0:T(8,128)} %get-tuple-element.11), kind=kLoop, calls=%fused_computation.16 | loop fusion | bytes 1024 | tf_op jit(solution)/shard_map/slice | solution.py:234
  87.6 22.4 %all-gather.1 = f32[8,1,256]{2,1,0:T(1,128)S(1)} all-gather(f32[1,1,256]{2,1,0:T(1,128)S(1)} %bitcast.47), channel_id=2, replica_groups=mesh['groups'=2,'tile'=4,'pair'=2,'sub'=2] {'tile','sub'}, dimensions={0}, use_global_device_ids=true | all-gather | bytes 9216 | tf_op jit(solution)/shard_map/all_gather | solution.py:235
  110.0 0.1 reshape.43
  110.1 0.1 reshape.44
  110.2 0.1 convert_reduce_fusion.1
  110.3 0.9 all-to-all-done
  111.2 0.5 abs_multiply_fusion
  111.7 2.3 %fusion = f32[32,4096]{1,0:T(8,128)S(1)} fusion(f32[16,8,32,128]{3,2,1,0:T(8,128)S(1)} %bitcast.38, f32[32]{0:T(128)S(1)} %broadcast_maximum_fusion, f32[128]{0:T(128)S(1)} %get-tuple-element.15, f32[128]{0:T(128)S(1)} %get-tuple-element.16), kind=kOutput, calls=%fused_computation.1 | convolution fusion | flops 201338880 | bytes 2622592 | tf_op jit(solution)/shard_map/dot_general | solution.py:245
  114.0 2.8 %collective-permute-start.1 = (f32[1,8,4096]{2,1,0:T(8,128)S(1)}, f32[1,8,4096]{2,1,0:T(8,128)S(1)}, u32[]{:S(2)}, u32[]{:S(2)}) collective-permute-start(f32[1,8,4096]{2,1,0:T(8,128)S(1)} %get-tuple-element.14), channel_id=1, source_target_pairs={{1,0},{4,1},{5,4},{8,5},{9,8},{12,9},{13,12},{3,2},{6,3},{7,6},{10... | collective-permute-start | bytes 393224 | tf_op jit(solution)/shard_map/ppermute | solution.py:31
  116.8 4.2 %collective-permute-start = (f32[1,8,4096]{2,1,0:T(8,128)S(1)}, f32[1,8,4096]{2,1,0:T(8,128)S(1)}, u32[]{:S(2)}, u32[]{:S(2)}) collective-permute-start(f32[1,8,4096]{2,1,0:T(8,128)S(1)} %get-tuple-element.13), channel_id=1, source_target_pairs={{0,1},{1,4},{4,5},{5,8},{8,9},{9,12},{12,13},{2,3},{3,6},{6,7},{7,... | collective-permute-start | bytes 393224 | tf_op jit(solution)/shard_map/ppermute | solution.py:28
  121.1 0.7 collective-permute-done.1
  121.8 1.2 collective-permute-done
  123.0 0.2 fusion.5
  123.2 0.8 reshape.47
  123.9 0.1 copy.31
  124.1 1.2 reshape.48
  (14 shorter events, 0.1 us)
Async XLA Ops:
  6.5 3.4 %copy-start = (bf16[1,64,16384]{2,1,0:T(8,128)(2,1)S(1)}, bf16[1,64,16384]{2,1,0:T(8,128)(2,1)}, u32[]{:S(2)}) copy-start(bf16[1,64,16384]{2,1,0:T(8,128)(2,1)} %param.5) | copy-start | bytes 6291460
  6.5 35.1 %all-gather.4.cloned.1.call-start = ((), (), s32[]{:S(2)}) async-start(), calls=%async_computation.1 | async-start | bytes 2359296 | tf_op jit(solution)/shard_map/all_gather | solution.py:210
  10.0 1.9 %copy-start.1 = (s32[1,64,1]{1,2,0:T(1,128)S(1)}, s32[1,64,1]{1,2,0:T(1,128)}, u32[]{:S(2)}) copy-start(s32[1,64,1]{1,2,0:T(1,128)} %param.6) | copy-start | bytes 772
  12.0 15.1 %copy-start.2 = (s32[1,64]{1,0:T(1,128)S(1)}, s32[1,64]{1,0:T(1,128)}, u32[]{:S(2)}) copy-start(s32[1,64]{1,0:T(1,128)} %param.7) | copy-start | bytes 772
  81.5 3.9 %copy-start.3 = (s32[64]{0:T(128)S(1)}, s32[64]{0:T(128)}, u32[]{:S(2)}) copy-start(s32[64]{0:T(128)} %get-tuple-element.18.places_ref) | copy-start | bytes 772
  81.5 29.7 %all-to-all-start = ((s16[128,32,128]{2,1,0:T(8,128)(2,1)}), s16[128,32,128]{2,1,0:T(8,128)(2,1)S(1)}, u32[]{:S(2)}, u32[]{:S(2)}) async-start(s16[128,32,128]{2,1,0:T(8,128)(2,1)} %get-tuple-element.12), calls=%async_computation | async-start | bytes 2097152 | tf_op jit(solution)/shard_map/all_to_all | solution.py:233
  114.0 7.8 %collective-permute-start.1 = (f32[1,8,4096]{2,1,0:T(8,128)S(1)}, f32[1,8,4096]{2,1,0:T(8,128)S(1)}, u32[]{:S(2)}, u32[]{:S(2)}) collective-permute-start(f32[1,8,4096]{2,1,0:T(8,128)S(1)} %get-tuple-element.14), channel_id=1, source_target_pairs={{1,0},{4,1},{5,4},{8,5},{9,8},{12,9},{13,12},{3,2},{6,3},{7,6},{10... | collective-permute-start | bytes 393224 | tf_op jit(solution)/shard_map/ppermute | solution.py:31
  116.8 6.2 %collective-permute-start = (f32[1,8,4096]{2,1,0:T(8,128)S(1)}, f32[1,8,4096]{2,1,0:T(8,128)S(1)}, u32[]{:S(2)}, u32[]{:S(2)}) collective-permute-start(f32[1,8,4096]{2,1,0:T(8,128)S(1)} %get-tuple-element.13), channel_id=1, source_target_pairs={{0,1},{1,4},{4,5},{5,8},{8,9},{9,12},{12,13},{2,3},{3,6},{6,7},{7,... | collective-permute-start | bytes 393224 | tf_op jit(solution)/shard_map/ppermute | solution.py:28
Sparse Core Ops, SparseCore 0:
  10.1 31.5 all-gather.3
